TPU v7x, 128 devices: a whole 4x4x4 slice. The times are simulated.
128 devices in a mesh: lat: 16 (over y, x_lo, core), ens: 8 (over z, x_hi).
Axes of the slice: x: 4 (x_hi: 2, x_lo: 2; x = x_hi * 2 + x_lo), y: 4, z: 4, core: 2. Of those that a mesh axis runs over, the one named last changes fastest.
Arguments:
- passed_on: float32 [8, 192, 16, 384], P('ens', None, None, 'lat'), may hold values from -6 to 6
- passed_grad: float32 [8, 192, 16, 384], P('ens', None, None, 'lat'), may hold values from -6 to 6
- latent: float32 [8, 192, 16, 384], P('ens', None, 'lat'), may hold values from -6 to 6
- mix_factors: float32 [2, 96, 96], replicated, may hold values from -0.25 to 0.25
- in_kernel: bfloat16 [2, 9, 48, 512], replicated, may hold values from -0.3125 to 0.3125
- in_bias: float32 [2, 512], replicated, may hold values from -3 to 3
- out_kernel: bfloat16 [2, 9, 96, 512], replicated, may hold values from -0.09375 to 0.09375
- out_bias: float32 [2, 96], replicated, may hold values from -3 to 3
Outputs:
- rebuilt: float32 [8, 96, 32, 768], P('ens', None, 'lat')
- input_grad: float32 [8, 96, 32, 768], P('ens', None, 'lat')
- mix_grad: float32 [2, 96, 96], replicated
- in_kernel_grad: float32 [2, 9, 48, 512], replicated
- in_bias_grad: float32 [2, 512], replicated
- out_kernel_grad: float32 [2, 9, 96, 512], replicated
- out_bias_grad: float32 [2, 96], replicated
All inputs are finite; a program needn't handle non-finite values.
Results may differ from a plain program's by a relative error of at most 0.0028.
Values may be sent and summed in bfloat16 or wider, within the bound.
No kernel may reach another device: no remote copies, remote signals or barrier semaphores. Data moves between devices by JAX's collectives and lax.ppermute only.
A program may use at most 192 MiB of HBM per device.

v0:
```python
import functools

import jax
import jax.numpy as jnp
from jax import lax
from jax.experimental import pallas as pl
from jax.experimental.pallas import tpu as pltpu
from jax.sharding import Mesh, PartitionSpec as P

BF = jnp.bfloat16
F32 = jnp.float32
HIGH = lax.Precision.HIGHEST
LAT = ("y", "xl", "c")
ENS = ("z", "xh")
CHIPS = ("y", "xl", "z", "xh")
HALF = 48
CH = 96
HID = 512
COLS = 384
ROW = 768
CELLS = 1536
PACK = 1536
VMEM_LIMIT = 56 * 1024 * 1024


def mm(a, b):
    return lax.dot_general(a, b, (((1,), (0,)), ((), ())), preferred_element_type=F32)


def mm_nt(a, b):
    return lax.dot_general(a, b, (((1,), (1,)), ((), ())), preferred_element_type=F32)


def mm_high(a, b):
    return lax.dot_general(
        a, b, (((1,), (0,)), ((), ())), preferred_element_type=F32, precision=HIGH
    )


def split3(x):
    hi = x.astype(BF)
    rest = x - hi.astype(F32)
    mid = rest.astype(BF)
    low = (rest - mid.astype(F32)).astype(BF)
    return hi, mid, low


def from_left(x):
    lane = lax.broadcasted_iota(jnp.int32, x.shape, 1)
    return jnp.where(lane == 0, 0.0, pltpu.roll(x, 1, 1))


def from_right(x):
    width = x.shape[1]
    lane = lax.broadcasted_iota(jnp.int32, x.shape, 1)
    return jnp.where(lane == width - 1, 0.0, pltpu.roll(x, width - 1, 1))


def call(body, outs, ins, scratch=(), smem=(), flops=0, name=None):
    in_specs = [
        pl.BlockSpec(memory_space=pltpu.SMEM if i in smem else pltpu.VMEM) for i in range(len(ins))
    ]
    moved = sum(x.size * x.dtype.itemsize for x in ins) + sum(
        x.size * x.dtype.itemsize for x in outs
    )
    return pl.pallas_call(
        body,
        out_shape=outs,
        in_specs=in_specs,
        out_specs=[pl.BlockSpec(memory_space=pltpu.VMEM) for _ in outs],
        scratch_shapes=list(scratch),
        compiler_params=pltpu.CompilerParams(vmem_limit_bytes=VMEM_LIMIT),
        cost_estimate=pl.CostEstimate(flops=flops, bytes_accessed=moved, transcendentals=0),
        name=name,
    )(*ins)


def sds(shape, dtype):
    return jax.ShapeDtypeStruct(shape, dtype)


def prep_kernel(mix_ref, w1_ref, w2_ref, inv_ref, lut_ref, w1t_ref, w2t_ref, w2k_ref):
    flows = mix_ref.shape[0]
    row = lax.broadcasted_iota(jnp.int32, (CH, CH), 0)
    col = lax.broadcasted_iota(jnp.int32, (CH, CH), 1)
    eye = (row == col).astype(F32)
    near = (row // 16) == (col // 16)
    units = []
    for k in range(flows):
        mix = mix_ref[k]
        units.append(jnp.where(row > col, mix, 0.0))
        units.append(jnp.where(row < col, mix, 0.0))
    inner = [jnp.where(near, u, 0.0) for u in units]
    outer = [u - i for u, i in zip(units, inner)]
    power = inner
    blocks = [eye - n for n in inner]
    for _ in range(3):
        power = [mm_high(p, p) for p in power]
        blocks = [mm_high(b, eye + p) for b, p in zip(blocks, power)]
    power = [mm_high(b, o) for b, o in zip(blocks, outer)]
    whole = [eye - p for p in power]
    for _ in range(2):
        power = [mm_high(p, p) for p in power]
        whole = [mm_high(w, eye + p) for w, p in zip(whole, power)]
    inverses = [mm_high(w, b) for w, b in zip(whole, blocks)]
    for k in range(flows):
        inv_ref[k] = mm_high(inverses[2 * k + 1], inverses[2 * k])
        lut_ref[k] = mm_high(units[2 * k] + eye, units[2 * k + 1] + eye).T
        for tap in range(9):
            w1t_ref[k, :, tap * HALF : (tap + 1) * HALF] = (
                w1_ref[k, tap].astype(F32).T.astype(BF)
            )
            w2t_ref[k, :, tap * CH : (tap + 1) * CH] = (
                w2_ref[k, 8 - tap].astype(F32).T.astype(BF)
            )
        for a in range(3):
            for b in range(3):
                w2k_ref[k, b * CH : (b + 1) * CH, a * HID : (a + 1) * HID] = w2_ref[k, 3 * a + b]


def prep(mix_factors, in_kernel, out_kernel):
    flows = mix_factors.shape[0]
    return call(
        prep_kernel,
        [
            sds((flows, CH, CH), F32),
            sds((flows, CH, CH), F32),
            sds((flows, HID, 9 * HALF), BF),
            sds((flows, HID, 9 * CH), BF),
            sds((flows, 3 * CH, 3 * HID), BF),
        ],
        [mix_factors, in_kernel, out_kernel],
        name="prep",
    )


def turn_kernel(recv_ref, above_ref, mid_ref, below_ref, ya_ref, ga_ref, stage):
    row = lax.broadcasted_iota(jnp.int32, (2 * CH, 2 * CH), 0)
    col = lax.broadcasted_iota(jnp.int32, (2 * CH, 2 * CH), 1)
    pick = (col == 4 * (row % HALF) + row // HALF).astype(BF)
    sources, kinds, width = recv_ref.shape[0], 6, recv_ref.shape[2]
    turned = []
    for kind in range(kinds):
        for s in range(sources):
            stage[s * width : (s + 1) * width, :] = recv_ref[s, kind].astype(F32)
        turned.append(mm_nt(pick, stage[...].astype(BF)))
    above_ref[...] = turned[0].astype(BF)
    mid_ref[...] = turned[1].astype(BF)
    below_ref[...] = turned[2].astype(BF)
    kept = turned[1] + turned[3]
    grad = turned[4] + turned[5]
    for k in range(4):
        ya_ref[:, k * COLS : (k + 1) * COLS] = kept[k * HALF : (k + 1) * HALF]
        ga_ref[:, k * COLS : (k + 1) * COLS] = grad[k * HALF : (k + 1) * HALF]


def turn(recv):
    return call(
        turn_kernel,
        [sds((2 * CH, COLS), BF)] * 3 + [sds((HALF, CELLS), F32)] * 2,
        [recv],
        scratch=[pltpu.VMEM((COLS, 2 * CH), F32)],
        name="turn",
    )


def stack_planes(even, odd):
    left = from_left(odd.astype(F32)).astype(BF)
    right = from_right(even.astype(F32)).astype(BF)
    return jnp.concatenate([left, even, odd, right], axis=0)


def fill_input_columns(above_ref, mid_ref, below_ref, columns, first, count):
    refs = {-2: (above_ref, 0), -1: (above_ref, CH), 0: (mid_ref, 0)}
    refs.update({1: (mid_ref, CH), 2: (below_ref, 0), 3: (below_ref, CH)})
    for source in range(first - 1, first + count + 1):
        ref, at = refs[source]
        stacked = stack_planes(ref[at : at + HALF], ref[at + HALF : at + CH])
        for a in range(3):
            target = source - a + 1 - first
            if 0 <= target < count:
                for p in range(2):
                    lane = (2 * target + p) * COLS
                    columns[a * 144 : (a + 1) * 144, lane : lane + COLS] = stacked[
                        p * HALF : p * HALF + 144
                    ]


def fill_grad_columns(top_ref, mid_ref, bottom_ref, columns):
    refs = [(top_ref, 0), (mid_ref, 0), (mid_ref, 2 * CH), (bottom_ref, 0)]
    for source in range(4):
        ref, at = refs[source]
        stacked = stack_planes(ref[at : at + CH], ref[at + CH : at + 2 * CH])
        for a in range(3):
            target = source - a
            if 0 <= target < 2:
                for p in range(2):
                    lane = (2 * target + p) * COLS
                    columns[a * 288 : (a + 1) * 288, lane : lane + COLS] = stacked[
                        p * CH : p * CH + 288
                    ]


def put_out_grad(raw, moved, out_ref):
    for r in range(2):
        for p in range(2):
            lane = (2 * r + p) * COLS
            at = (2 * r + p) * CH
            out_ref[at : at + HALF] = raw[:, lane : lane + COLS].astype(BF)
            out_ref[at + HALF : at + CH] = moved[:, lane : lane + COLS].astype(BF)


def forward_kernel(
    with_grad,
    flags_ref,
    above_ref,
    mid_ref,
    below_ref,
    w1t_ref,
    b1_ref,
    w2k_ref,
    b2_ref,
    inv_ref,
    ya_ref,
    yb_ref,
    x_ref,
    next_ref,
    scale_ref,
    hid_ref,
    slope_ref,
    *rest,
):
    if with_grad:
        grad_ref, moved_ref = rest[0], rest[1]
    columns, pre, rows, outs = rest[-4:]
    fill_input_columns(above_ref, mid_ref, below_ref, columns, -1, 4)
    bias = b1_ref[...]
    for h in range(4):
        pre[...] = mm(w1t_ref[...], columns[:, h * ROW : (h + 1) * ROW])
        inside = flags_ref[0] if h == 0 else flags_ref[1] if h == 3 else None

        def activate(step, carry):
            at = pl.multiple_of(step * 16, 16)
            value = pre[pl.ds(at, 16), :] + b1_ref[pl.ds(at, 16), :]
            gate = 0.5 + 0.5 * jnp.tanh(0.5 * value)
            hidden = value * gate
            if inside is not None:
                rows[pl.ds(h * HID + at, 16), :] = (hidden * inside).astype(BF)
            else:
                rows[pl.ds(h * HID + at, 16), :] = hidden.astype(BF)
                hid_ref[pl.ds((h - 1) * HID + at, 16), :] = hidden.astype(BF)
                slope_ref[pl.ds((h - 1) * HID + at, 16), :] = gate + hidden * (1.0 - gate)
            return carry

        lax.fori_loop(0, HID // 16, activate, 0)
    for r in range(2):
        taps = mm(w2k_ref[...], rows[r * HID : (r + 3) * HID, :])
        even, odd = taps[:, :COLS], taps[:, COLS:]
        lane = 2 * r * COLS
        outs[:, lane : lane + COLS] = from_left(odd[:CH]) + even[CH : 2 * CH] + odd[2 * CH :]
        outs[:, lane + COLS : lane + ROW] = even[:CH] + odd[CH : 2 * CH] + from_right(even[2 * CH :])
    raw = outs[:HALF] + b2_ref[:HALF]
    shift = outs[HALF:] + b2_ref[HALF:]
    inverse = 1.0 + jnp.exp(-(raw + 2.0))
    scale = 1.0 / inverse
    moved_in = yb_ref[...] * inverse - shift
    scale_ref[...] = scale
    x = mm_high(inv_ref[...], jnp.concatenate([ya_ref[...], moved_in], axis=0))
    x_ref[...] = x
    for k in range(4):
        next_ref[k * HALF : (k + 1) * HALF] = x[:HALF, k * COLS : (k + 1) * COLS].astype(BF)
    if with_grad:
        moved_grad = yb_ref[...]
        moved = moved_grad * scale
        moved_ref[...] = moved
        put_out_grad((moved_grad * yb_ref[...] - 1.0) * (1.0 - scale), moved, grad_ref)


def forward(flags, above, mid, below, w1t, b1, w2k, b2, inv, ya, yb, with_grad):
    outs = [
        sds((CH, CELLS), F32),
        sds((2 * CH, COLS), BF),
        sds((HALF, CELLS), F32),
        sds((2 * HID, ROW), BF),
        sds((2 * HID, ROW), F32),
    ]
    if with_grad:
        outs += [sds((4 * CH, COLS), BF), sds((HALF, CELLS), F32)]
    return call(
        functools.partial(forward_kernel, with_grad),
        outs,
        [flags, above, mid, below, w1t, b1, w2k, b2, inv, ya, yb],
        scratch=[
            pltpu.VMEM((9 * HALF, 4 * ROW), BF),
            pltpu.VMEM((HID, ROW), F32),
            pltpu.VMEM((4 * HID, ROW), BF),
            pltpu.VMEM((CH, CELLS), F32),
        ],
        smem=(0,),
        flops=4 * 10**9,
        name="forward",
    )


def backward_kernel(
    top_ref, mid_ref, bottom_ref, w2t_ref, slope_ref, w1_ref, gpre_ref, up_ref, in_ref, down_ref,
    columns, hid_grad, sums,
):
    fill_grad_columns(top_ref, mid_ref, bottom_ref, columns)
    sums[...] = jnp.zeros_like(sums)
    for r in range(2):
        hid_grad[...] = mm(w2t_ref[...], columns[:, r * ROW : (r + 1) * ROW])

        def slope(step, carry):
            at = pl.multiple_of(step * 16, 16)
            gpre_ref[pl.ds(r * HID + at, 16), :] = (
                hid_grad[pl.ds(at, 16), :] * slope_ref[pl.ds(r * HID + at, 16), :]
            ).astype(BF)
            return carry

        lax.fori_loop(0, HID // 16, slope, 0)
        taps = mm(w1_ref[...], gpre_ref[r * HID : (r + 1) * HID, :])
        for a in range(3):
            sums[r + a] += taps[a * 144 : (a + 1) * 144]
    for row, (ref, at) in enumerate(((up_ref, 0), (in_ref, 0), (in_ref, CH), (down_ref, 0))):
        total = sums[row]
        even, odd = total[:, :COLS], total[:, COLS:]
        b0, b1, b2 = slice(0, HALF), slice(HALF, CH), slice(CH, 3 * HALF)
        new_even = odd[b0] + even[b1] + from_left(odd[b2])
        new_odd = from_right(even[b0]) + odd[b1] + even[b2]
        ref[at : at + HALF] = new_even.astype(ref.dtype)
        ref[at + HALF : at + CH] = new_odd.astype(ref.dtype)


def backward(top, mid, bottom, w2t, slope, w1):
    return call(
        backward_kernel,
        [
            sds((2 * HID, ROW), BF),
            sds((CH, COLS), BF),
            sds((2 * CH, COLS), F32),
            sds((CH, COLS), BF),
        ],
        [top, mid, bottom, w2t, slope, w1],
        scratch=[
            pltpu.VMEM((9 * CH, CELLS), BF),
            pltpu.VMEM((HID, ROW), F32),
            pltpu.VMEM((4, 144, ROW), F32),
        ],
        flops=4 * 10**9,
        name="backward",
    )


def weight_kernel(
    above_ref, mid_ref, below_ref, top_ref, gmid_ref, bottom_ref, hid_ref, gpre_ref, out_ref,
    in_columns, grad_columns,
):
    fill_input_columns(above_ref, mid_ref, below_ref, in_columns, 0, 2)
    fill_grad_columns(top_ref, gmid_ref, bottom_ref, grad_columns)
    out_ref[:432] = mm_nt(in_columns[:, :ROW], gpre_ref[:HID]) + mm_nt(
        in_columns[:, ROW:], gpre_ref[HID:]
    )
    out_ref[432:1296] = mm_nt(grad_columns[:, :ROW], hid_ref[:HID]) + mm_nt(
        grad_columns[:, ROW:], hid_ref[HID:]
    )
    out_ref[1296:] = jnp.zeros((PACK - 1296, HID), F32)
    ones = jnp.ones((8, ROW), BF)
    out_ref[1392:1400] = mm_nt(ones, gpre_ref[:HID]) + mm_nt(ones, gpre_ref[HID:])
    own = slice(4 * CH, 5 * CH)
    out_ref[1400:1408, :CH] = mm_nt(ones, grad_columns[own, :ROW]) + mm_nt(
        ones, grad_columns[own, ROW:]
    )


def weight(above, mid, below, top, gmid, bottom, hid, gpre):
    return call(
        weight_kernel,
        [sds((PACK, HID), F32)],
        [above, mid, below, top, gmid, bottom, hid, gpre],
        scratch=[pltpu.VMEM((9 * HALF, CELLS), BF), pltpu.VMEM((9 * CH, CELLS), BF)],
        flops=4 * 10**9,
        name="weights",
    )[0]


def close_kernel(
    next_step, in_ref, low_ref, high_ref, ga_ref, moved_ref, lut_ref, x_ref, *rest
):
    if next_step:
        scale_ref, dmix_ref, gx_ref, grad_ref, nmoved_ref, whole = rest
    else:
        dmix_ref, gx_ref, whole = rest
    for k in range(4):
        part = in_ref[k * HALF : (k + 1) * HALF]
        if k < 2:
            part = part + low_ref[k * HALF : (k + 1) * HALF].astype(F32)
        else:
            part = part + high_ref[(k - 2) * HALF : (k - 1) * HALF].astype(F32)
        lane = k * COLS
        whole[:HALF, lane : lane + COLS] = ga_ref[:, lane : lane + COLS] + part
    whole[HALF:] = moved_ref[...]
    gx = mm_high(lut_ref[...], whole[...])
    gx_ref[...] = gx
    if next_step:
        scale = scale_ref[...]
        moved_grad = gx[HALF:]
        moved = moved_grad * scale
        nmoved_ref[...] = moved
        put_out_grad((moved_grad * x_ref[HALF:] - 1.0) * (1.0 - scale), moved, grad_ref)
    ghi, gmid, _ = split3(whole[...])
    xhi, xmid, _ = split3(x_ref[...])
    dmix_ref[...] = mm_nt(ghi, xhi) + (mm_nt(ghi, xmid) + mm_nt(gmid, xhi))


def close(gin, low, high, ga, moved, lut, x, scale=None):
    outs = [sds((CH, CH), F32), sds((CH, CELLS), F32)]
    ins = [gin, low, high, ga, moved, lut, x]
    if scale is not None:
        outs += [sds((4 * CH, COLS), BF), sds((HALF, CELLS), F32)]
        ins += [scale]
    return call(
        functools.partial(close_kernel, scale is not None),
        outs,
        ins,
        scratch=[pltpu.VMEM((CH, CELLS), F32)],
        flops=10**9,
        name="close",
    )


def weave_kernel(x_ref, out_ref):
    size = 256
    row = lax.broadcasted_iota(jnp.int32, (size, size), 0)
    col = lax.broadcasted_iota(jnp.int32, (size, size), 1)
    place = (col == 2 * (row % 128) + row // 128).astype(BF)
    for r in range(2):
        for t in range(3):
            lane = r * ROW + t * 128
            pair = jnp.concatenate(
                [x_ref[:, lane : lane + 128], x_ref[:, lane + COLS : lane + COLS + 128]], axis=1
            )
            hi, mid, low = split3(pair)
            woven = mm(hi, place) + (mm(mid, place) + mm(low, place))
            out_ref[0, :, r, t * size : (t + 1) * size] = woven


def weave(x):
    return call(weave_kernel, [sds((1, CH, 2, ROW), F32)], [x], name="weave")[0]


def triangle_grad(outer_sum, mix):
    eye = jnp.eye(CH, dtype=F32)
    lower = eye + jnp.tril(mix, -1)
    upper = eye + jnp.triu(mix, 1)
    low = jnp.tril(jnp.dot(outer_sum, upper.T, precision=HIGH), -1)
    high = jnp.triu(jnp.dot(lower.T, outer_sum, precision=HIGH), 1)
    return low + high


def local(passed_on, passed_grad, latent, mix_factors, in_kernel, in_bias, out_kernel, out_bias):
    lat_index = lax.axis_index(LAT)
    lat_count = lax.axis_size(LAT)
    forth = [(i, i + 1) for i in range(lat_count - 1)]
    back = [(i + 1, i) for i in range(lat_count - 1)]
    flags = jnp.stack([lat_index > 0, lat_index < lat_count - 1]).astype(F32)

    on = jnp.transpose(passed_on[0], (1, 2, 0))
    grad = jnp.transpose(passed_grad[0], (1, 2, 0))
    on_hi = on.astype(BF)
    on_lo = (on - on_hi.astype(F32)).astype(BF)
    grad_hi = grad.astype(BF)
    grad_lo = (grad - grad_hi.astype(F32)).astype(BF)
    blank = jnp.zeros_like(on_hi[:1])
    payload = jnp.stack(
        [
            jnp.concatenate([blank, on_hi[:-1]]),
            on_hi,
            jnp.concatenate([on_hi[1:], blank]),
            on_lo,
            grad_hi,
            grad_lo,
        ],
        axis=1,
    )
    recv = lax.all_to_all(payload, LAT, 0, 0, tiled=True)
    inv, lut, w1t, w2t, w2k = prep(mix_factors, in_kernel, out_kernel)
    w1 = in_kernel.reshape(2, 9 * HALF, HID)
    yb = latent.reshape(HALF, 4, COLS).reshape(HALF, CELLS)
    b1 = in_bias[:, :, None]
    b2 = out_bias[:, :, None]

    above, mid, below, ya, ga = turn(recv)
    x1, next_mid, _, hid1, slope1, grad1, moved1 = forward(
        flags, above, mid, below, w1t[1], b1[1], w2k[1], b2[1], inv[1], ya, yb, True
    )
    gtop = lax.ppermute(grad1[2 * CH :], LAT, forth)
    gbottom = lax.ppermute(grad1[: 2 * CH], LAT, back)
    above0 = lax.ppermute(next_mid, LAT, forth)
    below0 = lax.ppermute(next_mid, LAT, back)
    gpre1, up1, in1, down1 = backward(gtop, grad1, gbottom, w2t[1], slope1, w1[1])
    low1 = lax.ppermute(down1, LAT, forth)
    high1 = lax.ppermute(up1, LAT, back)
    x0, _, scale0, hid0, slope0 = forward(
        flags, above0, next_mid, below0, w1t[0], b1[0], w2k[0], b2[0], inv[0],
        x1[:HALF], x1[HALF:], False,
    )
    dmix1, gx1, grad0, moved0 = close(in1, low1, high1, ga, moved1, lut[1], x1, scale0)
    gtop0 = lax.ppermute(grad0[2 * CH :], LAT, forth)
    gbottom0 = lax.ppermute(grad0[: 2 * CH], LAT, back)
    pack1 = weight(above, mid, below, gtop, grad1, gbottom, hid1, gpre1)
    rebuilt = weave(x0)
    gpre0, up0, in0, down0 = backward(gtop0, grad0, gbottom0, w2t[0], slope0, w1[0])
    low0 = lax.ppermute(down0, LAT, forth)
    high0 = lax.ppermute(up0, LAT, back)
    pack0 = weight(above0, next_mid, below0, gtop0, grad0, gbottom0, hid0, gpre0)
    dmix0, gx0 = close(in0, low0, high0, gx1[:HALF], moved0, lut[0], x0)
    input_grad = weave(gx0)

    def place(pack, dmix):
        return lax.dynamic_update_slice(pack, dmix, (1296, 0))

    pack0 = place(pack0, dmix0)
    pack1 = place(pack1, dmix1)
    is_one = lax.axis_index("c") == 1
    keep = jnp.where(is_one, pack1, pack0)
    give = jnp.where(is_one, pack0, pack1)
    swap = [(0, 1), (1, 0)]
    got = lax.ppermute(give, "c", swap)
    chips = lax.axis_size(CHIPS)
    total = (keep + got).astype(BF).reshape(chips, PACK // chips, HID)
    shares = lax.all_to_all(total, CHIPS, 0, 0, tiled=True)
    cells = float(CELLS * lat_count * lax.axis_size(ENS))
    share = (jnp.sum(shares.astype(F32), axis=0, keepdims=True) / cells).astype(BF)
    spread = jnp.broadcast_to(share, (chips, PACK // chips, HID))
    mine = lax.all_to_all(spread, CHIPS, 0, 0, tiled=True).reshape(PACK, HID)
    other = lax.ppermute(mine, "c", swap)
    sums = jnp.stack([jnp.where(is_one, other, mine), jnp.where(is_one, mine, other)]).astype(F32)
    mix_grad = jnp.stack(
        [triangle_grad(sums[k, 1296:1392, :CH], mix_factors[k]) for k in range(2)]
    )
    return (
        rebuilt,
        input_grad,
        mix_grad,
        sums[:, :432].reshape(2, 9, HALF, HID),
        sums[:, 1392],
        sums[:, 432:1296].reshape(2, 9, CH, HID)[:, ::-1],
        sums[:, 1400, :CH],
    )


def solution(mesh):
    split = Mesh(mesh.devices.reshape(4, 2, 2, 4, 2), ("y", "xl", "c", "z", "xh"))
    return jax.shard_map(
        local,
        mesh=split,
        in_specs=(
            P(ENS, None, None, LAT),
            P(ENS, None, None, LAT),
            P(ENS, None, LAT, None),
            P(),
            P(),
            P(),
            P(),
            P(),
        ),
        out_specs=(P(ENS, None, LAT, None), P(ENS, None, LAT, None), P(), P(), P(), P(), P()),
        check_vma=False,
    )
```

profile of v0, /device:TPU:1, one launch (start us, length us, event | category | flops | bytes accessed | tf_op | source)
XLA Modules:
  0.0 249.6 jit_solution(9652356873202600672)
XLA Ops:
  6.1 7.0 %all-to-all-start = ((bf16[16,6,24,192]{3,2,1,0:T(8,128)(2,1)}), bf16[16,6,24,192]{3,2,1,0:T(8,128)(2,1)S(1)}, u32[]{:S(2)}, u32[]{:S(2)}) async-start(bf16[16,6,24,192]{3,2,1,0:T(8,128)(2,1)} %fusion.9), calls=%async_computation | async-start | bytes 2359296 | tf_op jit(solution)/shard_map/all_to_all | solution.py:486
  18.8 8.2 %prep.1 = (f32[2,96,96]{2,1,0:T(8,128)}, f32[2,96,96]{2,1,0:T(8,128)}, bf16[2,512,432]{2,1,0:T(8,128)(2,1)}, bf16[2,512,864]{2,1,0:T(8,128)(2,1)}, bf16[2,288,1536]{2,1,0:T(8,128)(2,1)}) custom-call(f32[2,96,96]{2,1,0:T(8,128)} %mix_ref.1, bf16[2,9,48,512]{3,2,1,0:T(8,128)(2,1)} %w1_ref.1, bf16[2,9,96,512]{3,2,1,0:T(8,128)(2,1)} %w2_ref.1), custom_call_target="tpu_custom_call" | custom-call | bytes 7299072 | tf_op jit(solution)/shard_map/prep/pallas_call | solution.py:66
  27.1 2.4 slice_bitcast_fusion.4
  35.8 2.7 %turn.1 = (bf16[192,384]{1,0:T(8,128)(2,1)}, bf16[192,384]{1,0:T(8,128)(2,1)}, bf16[192,384]{1,0:T(8,128)(2,1)}, f32[48,1536]{1,0:T(8,128)}, f32[48,1536]{1,0:T(8,128)}) custom-call(bf16[16,6,24,192]{3,2,1,0:T(8,128)(2,1)} %copy-done.2), custom_call_target="tpu_custom_call" | custom-call | bytes 1916928 | tf_op jit(solution)/shard_map/turn/pallas_call | solution.py:66
  38.5 20.4 %forward.2 = (f32[96,1536]{1,0:T(8,128)}, bf16[192,384]{1,0:T(8,128)(2,1)}, f32[48,1536]{1,0:T(8,128)}, bf16[1024,768]{1,0:T(8,128)(2,1)}, f32[1024,768]{1,0:T(8...) custom-call(f32[2]{0:T(128)} %add_convert_fusion.1.flags_ref, bf16[192,384]{1,0:T(8,128)(2,1)} %get-tuple-element.41.above_ref, ...), custom_call_target="tpu_custom_call" | custom-call | flops 4000000000 | bytes 8739208 | tf_op jit(solution)/shard_map/forward/pallas_call | solution.py:66
  58.9 2.0 collective-permute-start.1
  60.9 3.5 %collective-permute-start = (bf16[192,384]{1,0:T(8,128)(2,1)}, bf16[192,384]{1,0:T(8,128)(2,1)S(1)}, u32[]{:S(2)}, u32[]{:S(2)}) collective-permute-start(bf16[192,384]{1,0:T(8,128)(2,1)} %get-tuple-element.48.mid_ref), channel_id=1, source_target_pairs={{0,8},{8,16},{16,24},{24,32},{32,40},{40,48},{48,56},{56,64},{64,7... | collective-permute-start | bytes 442376 | tf_op jit(solution)/shard_map/ppermute | solution.py:499
  65.5 1.9 collective-permute-start.3
  67.4 3.8 %collective-permute-start.2 = (bf16[192,384]{1,0:T(8,128)(2,1)S(1)}, bf16[192,384]{1,0:T(8,128)(2,1)S(1)}, u32[]{:S(2)}, u32[]{:S(2)}) collective-permute-start(bf16[192,384]{1,0:T(8,128)(2,1)S(1)} %get-tuple-element.90), channel_id=1, source_target_pairs={{0,8},{8,16},{16,24},{24,32},{32,40},{40,48},{48,56},{56,64},{64,7... | collective-permute-start | bytes 442376 | tf_op jit(solution)/shard_map/ppermute | solution.py:497
  71.2 1.9 fusion.37
  73.9 7.7 %backward.2 = (bf16[1024,768]{1,0:T(8,128)(2,1)}, bf16[96,384]{1,0:T(8,128)(2,1)}, f32[192,384]{1,0:T(8,128)}, bf16[96,384]{1,0:T(8,128)(2,1)}) custom-call(bf16[192,384]{1,0:T(8,128)(2,1)} %copy-done.19, bf16[384,384]{1,0:T(8,128)(2,1)} %get-tuple-element.51.mid_ref.gmid_ref, bf16[192,384]{1,0:T(8,128)(2,1)} %copy-done.18, ...), custom_call_target="tpu_custom_call" | custom-call | flops 4000000000 | bytes 7077888 | tf_op jit(solution)/shard_map/backward/pallas_call | solution.py:66
  81.6 4.3 %collective-permute-start.4 = (bf16[96,384]{1,0:T(8,128)(2,1)}, bf16[96,384]{1,0:T(8,128)(2,1)S(1)}, u32[]{:S(2)}, u32[]{:S(2)}) collective-permute-start(bf16[96,384]{1,0:T(8,128)(2,1)} %get-tuple-element.55), channel_id=1, source_target_pairs={{0,8},{8,16},{16,24},{24,32},{32,40},{40,48},{48,56},{56,64},{64,7... | collective-permute-start | bytes 221192 | tf_op jit(solution)/shard_map/ppermute | solution.py:502
  85.8 1.9 collective-permute-start.5
  88.5 20.2 %forward.3 = (f32[96,1536]{1,0:T(8,128)}, bf16[192,384]{1,0:T(8,128)(2,1)}, f32[48,1536]{1,0:T(8,128)}, bf16[1024,768]{1,0:T(8,128)(2,1)}, f32[1024,768]{1,0:T(8,128)}) custom-call(f32[2]{0:T(128)} %add_convert_fusion.1.flags_ref, bf16[192,384]{1,0:T(8,128)(2,1)} %copy-done.17, bf16[192,384]{1,0:T(8,128)(2,1)} %get-tuple-element.48.mid_ref, ...), custom_call_target="tpu_custom_call" | custom-call | flops 4000000000 | bytes 8149384 | tf_op jit(solution)/shard_map/forward/pallas_call | solution.py:66
  109.4 3.4 %close.2 = (f32[96,96]{1,0:T(8,128)}, f32[96,1536]{1,0:T(8,128)}, bf16[384,384]{1,0:T(8,128)(2,1)}, f32[48,1536]{1,0:T(8,128)}) custom-call(f32[192,384]{1,0:T(8,128)} %get-tuple-element.54.in_ref, bf16[96,384]{1,0:T(8,128)(2,1)} %copy-done.22, bf16[96,384]{1,0:T(8,128)(2,1)} %copy-done.23, f32[48,1536]{1,0:T(8,128)} %get-tuple-element.57.ga_ref, ...), custom_call_target="tpu_custom_call" | custom-call | flops 1000000000 | bytes 3170304 | tf_op jit(solution)/shard_map/close/pallas_call | solution.py:66
  113.8 1.9 collective-permute-start.7
  115.7 3.9 %collective-permute-start.6 = (bf16[192,384]{1,0:T(8,128)(2,1)S(1)}, bf16[192,384]{1,0:T(8,128)(2,1)S(1)}, u32[]{:S(2)}, u32[]{:S(2)}) collective-permute-start(bf16[192,384]{1,0:T(8,128)(2,1)S(1)} %get-tuple-element.88), channel_id=1, source_target_pairs={{0,8},{8,16},{16,24},{24,32},{32,40},{40,48},{48,56},{56,64},{64,7... | collective-permute-start | bytes 442376 | tf_op jit(solution)/shard_map/ppermute | solution.py:509
  119.6 6.7 %weights.2 = f32[1536,512]{1,0:T(8,128)} custom-call(bf16[192,384]{1,0:T(8,128)(2,1)} %get-tuple-element.41.above_ref, bf16[192,384]{1,0:T(8,128)(2,1)} %get-tuple-element.42.mid_ref, bf16[192,384]{1,0:T(8,128)(2,1)} %get-tuple-element.43.below_ref, bf16[192,384]{1,0:T(8,128)(2,1)} %copy-done.19, bf16[384,384]{1,0:T(8,128)(2,1)} %get-tuple-element.51.mid_ref.gmid_ref, ...), custom_call_target="tpu_custom_call" | custom-call | flops 4000000000 | bytes 7323648 | tf_op jit(solution)/shard_map/weights/pallas_call | solution.py:66
  127.0 2.9 %dynamic_update_slice.6 = f32[1536,512]{1,0:T(8,128)} dynamic-update-slice(f32[1536,512]{1,0:T(8,128)} %weights.2, f32[96,96]{1,0:T(8,128)S(1)} %copy-done.13, s32[]{:T(128)} %constant.47.clone.1, s32[]{:T(128)} %constant.42.clone.1) | dynamic-update-slice | bytes 73732 | tf_op jit(solution)/shard_map/dynamic_update_slice | solution.py:521
  130.7 7.7 %backward.3 = (bf16[1024,768]{1,0:T(8,128)(2,1)}, bf16[96,384]{1,0:T(8,128)(2,1)}, f32[192,384]{1,0:T(8,128)}, bf16[96,384]{1,0:T(8,128)(2,1)}) custom-call(bf16[192,384]{1,0:T(8,128)(2,1)} %copy-done.21, bf16[384,384]{1,0:T(8,128)(2,1)} %get-tuple-element.61.mid_ref.gmid_ref, bf16[192,384]{1,0:T(8,128)(2,1)} %copy-done.20, ...), custom_call_target="tpu_custom_call" | custom-call | flops 4000000000 | bytes 7077888 | tf_op jit(solution)/shard_map/backward/pallas_call | solution.py:66
  138.3 4.6 %collective-permute-start.8 = (bf16[96,384]{1,0:T(8,128)(2,1)}, bf16[96,384]{1,0:T(8,128)(2,1)S(1)}, u32[]{:S(2)}, u32[]{:S(2)}) collective-permute-start(bf16[96,384]{1,0:T(8,128)(2,1)} %get-tuple-element.64), channel_id=1, source_target_pairs={{0,8},{8,16},{16,24},{24,32},{32,40},{40,48},{48,56},{56,64},{64,7... | collective-permute-start | bytes 221192 | tf_op jit(solution)/shard_map/ppermute | solution.py:514
  143.0 1.9 collective-permute-start.9
  144.9 6.7 %weights.3 = f32[1536,512]{1,0:T(8,128)} custom-call(bf16[192,384]{1,0:T(8,128)(2,1)} %copy-done.17, bf16[192,384]{1,0:T(8,128)(2,1)} %get-tuple-element.48.mid_ref, bf16[192,384]{1,0:T(8,128)(2,1)} %copy-done.16, bf16[192,384]{1,0:T(8,128)(2,1)} %copy-done.21, bf16[384,384]{1,0:T(8,128)(2,1)} %get-tuple-element.61.mid_ref.gmid_ref, ...), custom_call_target="tpu_custom_call" | custom-call | flops 4000000000 | bytes 7323648 | tf_op jit(solution)/shard_map/weights/pallas_call | solution.py:66
  152.3 3.2 %close.3 = (f32[96,96]{1,0:T(8,128)}, f32[96,1536]{1,0:T(8,128)}) custom-call(f32[192,384]{1,0:T(8,128)} %get-tuple-element.63.in_ref, bf16[96,384]{1,0:T(8,128)(2,1)} %copy-done.24, bf16[96,384]{1,0:T(8,128)(2,1)} %copy-done.25, f32[48,1536]{1,0:T(8,128)} %slice.130.ga_ref, f32[48,1536]{1,0:T(8,128)} %get-tuple-element.67.moved_ref, ...), custom_call_target="tpu_custom_call" | custom-call | flops 1000000000 | bytes 2285568 | tf_op jit(solution)/shard_map/close/pallas_call | solution.py:66
  155.5 2.3 dynamic_update_slice.7
  158.7 5.6 %collective-permute-done.10 = f32[1536,512]{1,0:T(8,128)S(1)} collective-permute-done((f32[1536,512]{1,0:T(8,128)S(1)}, f32[1536,512]{1,0:T(8,128)S(1)}, u32[]{:S(2)}, u32[]{:S(2)}) %collective-permute-start.10) | collective-permute-done | bytes 3145760 | tf_op jit(solution)/shard_map/ppermute | solution.py:529
  165.6 37.7 %all_to_all.15 = bf16[64,24,512]{2,1,0:T(8,128)(2,1)S(1)} all-to-all(bf16[64,24,512]{2,1,0:T(8,128)(2,1)S(1)} %bitcast.126), channel_id=1, replica_groups=mesh['y'=4,'xl'=2,'c'=2,'z'=4,'xh'=2] {'y','xl','z','xh'}, dimensions={0} | all-to-all | bytes 3145728 | tf_op jit(solution)/shard_map/all_to_all | solution.py:532
  203.7 25.9 %all_to_all.16 = bf16[64,24,512]{2,1,0:T(8,128)(2,1)S(1)} all-to-all(bf16[64,24,512]{2,1,0:T(8,128)(2,1)S(1)} %broadcast_in_dim.23), channel_id=1, replica_groups=mesh['y'=4,'xl'=2,'c'=2,'z'=4,'xh'=2] {'y','xl','z','xh'}, dimensions={0} | all-to-all | bytes 3145728 | tf_op jit(solution)/shard_map/all_to_all | solution.py:536
  229.6 4.5 %collective-permute-start.11 = (bf16[1536,512]{1,0:T(8,128)(2,1)S(1)}, bf16[1536,512]{1,0:T(8,128)(2,1)S(1)}, u32[]{:S(2)}, u32[]{:S(2)}) collective-permute-start(bf16[1536,512]{1,0:T(8,128)(2,1)S(1)} %bitcast.125), channel_id=1, source_target_pairs={{0,8},{8,0},{1,9},{9,1},{2,10},{10,2},{3,11},{11,3},{4,12},{12,4},... | collective-permute-start | bytes 4718600 | tf_op jit(solution)/shard_map/ppermute | solution.py:537
  234.1 2.5 weave.2
  236.6 2.5 weave.3
  245.8 2.3 rev.3
  (108 shorter events, 34.3 us)
Async XLA Ops:
  0.6 1.9 copy-start.3
  0.6 4.0 %copy-start.7 = (f32[1,192,16,24]{1,3,2,0:T(8,128)S(1)}, f32[1,192,16,24]{1,3,2,0:T(8,128)}, u32[]{:S(2)}) copy-start(f32[1,192,16,24]{1,3,2,0:T(8,128)} %param.9) | copy-start | bytes 884740
  5.4 7.8 %copy-start.15 = (f32[2,96]{1,0:T(2,128)S(1)}, f32[2,96]{1,0:T(2,128)}, u32[]{:S(2)}) copy-start(f32[2,96]{1,0:T(2,128)} %param.15) | copy-start | bytes 2308
  5.4 7.8 %copy-start.14 = (f32[2,512]{1,0:T(2,128)S(1)}, f32[2,512]{1,0:T(2,128)}, u32[]{:S(2)}) copy-start(f32[2,512]{1,0:T(2,128)} %param.13) | copy-start | bytes 12292
  6.1 10.3 %copy-start.9 = (f32[1,192,1,384]{3,2,1,0:T(1,128)S(1)}, f32[1,192,1,384]{3,2,1,0:T(1,128)}, u32[]{:S(2)}) copy-start(f32[1,192,1,384]{3,2,1,0:T(1,128)} %param.10) | copy-start | bytes 884740
  6.1 11.7 %copy-start.4 = (bf16[2,9,48,512]{3,2,1,0:T(8,128)(2,1)S(1)}, bf16[2,9,48,512]{3,2,1,0:T(8,128)(2,1)}, u32[]{:S(2)}) copy-start(bf16[2,9,48,512]{3,2,1,0:T(8,128)(2,1)} %w1_ref.1) | copy-start | bytes 2654212
  6.1 28.7 %all-to-all-start = ((bf16[16,6,24,192]{3,2,1,0:T(8,128)(2,1)}), bf16[16,6,24,192]{3,2,1,0:T(8,128)(2,1)S(1)}, u32[]{:S(2)}, u32[]{:S(2)}) async-start(bf16[16,6,24,192]{3,2,1,0:T(8,128)(2,1)} %fusion.9), calls=%async_computation | async-start | bytes 2359296 | tf_op jit(solution)/shard_map/all_to_all | solution.py:486
  27.0 2.4 copy-start.12
  27.0 3.1 %copy-start.11 = (f32[2,96,96]{2,1,0:T(8,128)S(1)}, f32[2,96,96]{2,1,0:T(8,128)}, u32[]{:S(2)}) copy-start(f32[2,96,96]{2,1,0:T(8,128)} %get-tuple-element.59) | copy-start | bytes 221188
  27.0 4.3 %copy-start.5 = (bf16[2,512,864]{2,1,0:T(8,128)(2,1)S(1)}, bf16[2,512,864]{2,1,0:T(8,128)(2,1)}, u32[]{:S(2)}) copy-start(bf16[2,512,864]{2,1,0:T(8,128)(2,1)} %get-tuple-element.52) | copy-start | bytes 5308420
  31.3 2.1 copy-start.6
  34.8 1.0 copy-start.2
  58.9 28.9 %collective-permute-start.1 = (bf16[192,384]{1,0:T(8,128)(2,1)}, bf16[192,384]{1,0:T(8,128)(2,1)S(1)}, u32[]{:S(2)}, u32[]{:S(2)}) collective-permute-start(bf16[192,384]{1,0:T(8,128)(2,1)} %get-tuple-element.48.mid_ref), channel_id=1, source_target_pairs={{8,0},{16,8},{24,16},{32,24},{40,32},{48,40},{56,48},{64,56},{72,6... | collective-permute-start | bytes 442376 | tf_op jit(solution)/shard_map/ppermute | solution.py:500
  60.9 26.9 %collective-permute-start = (bf16[192,384]{1,0:T(8,128)(2,1)}, bf16[192,384]{1,0:T(8,128)(2,1)S(1)}, u32[]{:S(2)}, u32[]{:S(2)}) collective-permute-start(bf16[192,384]{1,0:T(8,128)(2,1)} %get-tuple-element.48.mid_ref), channel_id=1, source_target_pairs={{0,8},{8,16},{16,24},{24,32},{32,40},{40,48},{48,56},{56,64},{64,7... | collective-permute-start | bytes 442376 | tf_op jit(solution)/shard_map/ppermute | solution.py:499
  65.5 7.7 %collective-permute-start.3 = (bf16[192,384]{1,0:T(8,128)(2,1)S(1)}, bf16[192,384]{1,0:T(8,128)(2,1)S(1)}, u32[]{:S(2)}, u32[]{:S(2)}) collective-permute-start(bf16[192,384]{1,0:T(8,128)(2,1)S(1)} %get-tuple-element.89), channel_id=1, source_target_pairs={{8,0},{16,8},{24,16},{32,24},{40,32},{48,40},{56,48},{64,56},{72,6... | collective-permute-start | bytes 442376 | tf_op jit(solution)/shard_map/ppermute | solution.py:498
  67.4 5.8 %collective-permute-start.2 = (bf16[192,384]{1,0:T(8,128)(2,1)S(1)}, bf16[192,384]{1,0:T(8,128)(2,1)S(1)}, u32[]{:S(2)}, u32[]{:S(2)}) collective-permute-start(bf16[192,384]{1,0:T(8,128)(2,1)S(1)} %get-tuple-element.90), channel_id=1, source_target_pairs={{0,8},{8,16},{16,24},{24,32},{32,40},{40,48},{48,56},{56,64},{64,7... | collective-permute-start | bytes 442376 | tf_op jit(solution)/shard_map/ppermute | solution.py:497
  73.2 0.7 copy-start.19
  81.6 27.2 %collective-permute-start.4 = (bf16[96,384]{1,0:T(8,128)(2,1)}, bf16[96,384]{1,0:T(8,128)(2,1)S(1)}, u32[]{:S(2)}, u32[]{:S(2)}) collective-permute-start(bf16[96,384]{1,0:T(8,128)(2,1)} %get-tuple-element.55), channel_id=1, source_target_pairs={{0,8},{8,16},{16,24},{24,32},{32,40},{40,48},{48,56},{56,64},{64,7... | collective-permute-start | bytes 221192 | tf_op jit(solution)/shard_map/ppermute | solution.py:502
  85.8 22.9 %collective-permute-start.5 = (bf16[96,384]{1,0:T(8,128)(2,1)}, bf16[96,384]{1,0:T(8,128)(2,1)S(1)}, u32[]{:S(2)}, u32[]{:S(2)}) collective-permute-start(bf16[96,384]{1,0:T(8,128)(2,1)} %get-tuple-element.56), channel_id=1, source_target_pairs={{8,0},{16,8},{24,16},{32,24},{40,32},{48,40},{56,48},{64,56},{72,6... | collective-permute-start | bytes 221192 | tf_op jit(solution)/shard_map/ppermute | solution.py:503
  87.8 0.7 copy-start.17
  113.8 16.1 %collective-permute-start.7 = (bf16[192,384]{1,0:T(8,128)(2,1)S(1)}, bf16[192,384]{1,0:T(8,128)(2,1)S(1)}, u32[]{:S(2)}, u32[]{:S(2)}) collective-permute-start(bf16[192,384]{1,0:T(8,128)(2,1)S(1)} %get-tuple-element.87), channel_id=1, source_target_pairs={{8,0},{16,8},{24,16},{32,24},{40,32},{48,40},{56,48},{64,56},{72,6... | collective-permute-start | bytes 442376 | tf_op jit(solution)/shard_map/ppermute | solution.py:510
  115.7 14.2 %collective-permute-start.6 = (bf16[192,384]{1,0:T(8,128)(2,1)S(1)}, bf16[192,384]{1,0:T(8,128)(2,1)S(1)}, u32[]{:S(2)}, u32[]{:S(2)}) collective-permute-start(bf16[192,384]{1,0:T(8,128)(2,1)S(1)} %get-tuple-element.88), channel_id=1, source_target_pairs={{0,8},{8,16},{16,24},{24,32},{32,40},{40,48},{48,56},{56,64},{64,7... | collective-permute-start | bytes 442376 | tf_op jit(solution)/shard_map/ppermute | solution.py:509
  119.6 6.7 %copy-start.10 = (f32[96,1536]{1,0:T(8,128)S(1)}, f32[96,1536]{1,0:T(8,128)}, u32[]{:S(2)}) copy-start(f32[96,1536]{1,0:T(8,128)} %get-tuple-element.66) | copy-start | bytes 1769476
  119.6 7.5 %copy-start.13 = (f32[96,96]{1,0:T(8,128)S(1)}, f32[96,96]{1,0:T(8,128)}, u32[]{:S(2)}) copy-start(f32[96,96]{1,0:T(8,128)} %get-tuple-element.71) | copy-start | bytes 110596
  129.9 0.7 copy-start.21
  138.3 13.3 %collective-permute-start.8 = (bf16[96,384]{1,0:T(8,128)(2,1)}, bf16[96,384]{1,0:T(8,128)(2,1)S(1)}, u32[]{:S(2)}, u32[]{:S(2)}) collective-permute-start(bf16[96,384]{1,0:T(8,128)(2,1)} %get-tuple-element.64), channel_id=1, source_target_pairs={{0,8},{8,16},{16,24},{24,32},{32,40},{40,48},{48,56},{56,64},{64,7... | collective-permute-start | bytes 221192 | tf_op jit(solution)/shard_map/ppermute | solution.py:514
  143.0 8.6 %collective-permute-start.9 = (bf16[96,384]{1,0:T(8,128)(2,1)}, bf16[96,384]{1,0:T(8,128)(2,1)S(1)}, u32[]{:S(2)}, u32[]{:S(2)}) collective-permute-start(bf16[96,384]{1,0:T(8,128)(2,1)} %get-tuple-element.65), channel_id=1, source_target_pairs={{8,0},{16,8},{24,16},{32,24},{40,32},{48,40},{56,48},{64,56},{72,6... | collective-permute-start | bytes 221192 | tf_op jit(solution)/shard_map/ppermute | solution.py:515
  152.3 3.2 %copy-start = (f32[1536,512]{1,0:T(8,128)S(1)}, f32[1536,512]{1,0:T(8,128)}, u32[]{:S(2)}) copy-start(f32[1536,512]{1,0:T(8,128)} %weights.3) | copy-start | bytes 9437188
  157.8 6.5 %copy-start.1 = (f32[1536,512]{1,0:T(8,128)S(1)}, f32[1536,512]{1,0:T(8,128)}, u32[]{:S(2)}) copy-start(f32[1536,512]{1,0:T(8,128)} %dynamic_update_slice.6) | copy-start | bytes 9437188
  158.6 5.7 %collective-permute-start.10 = (f32[1536,512]{1,0:T(8,128)S(1)}, f32[1536,512]{1,0:T(8,128)S(1)}, u32[]{:S(2)}, u32[]{:S(2)}) collective-permute-start(f32[1536,512]{1,0:T(8,128)S(1)} %broadcast_select_fusion), channel_id=1, source_target_pairs={{0,8},{8,0},{1,9},{9,1},{2,10},{10,2},{3,11},{11,3},{4,12},{12,4},... | collective-permute-start | bytes 9437192 | tf_op jit(solution)/shard_map/ppermute | solution.py:529
  229.6 9.5 %collective-permute-start.11 = (bf16[1536,512]{1,0:T(8,128)(2,1)S(1)}, bf16[1536,512]{1,0:T(8,128)(2,1)S(1)}, u32[]{:S(2)}, u32[]{:S(2)}) collective-permute-start(bf16[1536,512]{1,0:T(8,128)(2,1)S(1)} %bitcast.125), channel_id=1, source_target_pairs={{0,8},{8,0},{1,9},{9,1},{2,10},{10,2},{3,11},{11,3},{4,12},{12,4},... | collective-permute-start | bytes 4718600 | tf_op jit(solution)/shard_map/ppermute | solution.py:537
  239.9 0.9 copy-start.8
  (7 other events, 4.5 us)
where the time goes:
time: 251 us; the launch traced here: 250 us
  Pallas kernels  91.8 us (37%)
  blocking collectives  63.6 us (25%)
  starting transfers between devices  41.5 us (17%)
  local copies, waits for them, and re-layouts  33.5 us (13%)
  other arithmetic  10.3 us (4%)
  waiting for transfers between devices  5.68 us (2%)
    pallas_call x12, Pallas kernels, call(): pl.pallas_call(body, out_shape=outs, in_specs=in_specs, out_specs=[pl.Blo...  91.8 us
    all_to_all x1, blocking collectives, local(): shares = lax.all_to_all(total, CHIPS, 0, 0, tiled=True)  37.7 us
    all_to_all x1, blocking collectives, local(): mine = lax.all_to_all(spread, CHIPS, 0, 0, tiled=True).reshape(PACK, HID)  25.9 us
    unnamed x55, local copies, waits for them, and re-layouts  8.14 us
    all_to_all x1, starting transfers between devices, local(): recv = lax.all_to_all(payload, LAT, 0, 0, tiled=True)  7.05 us
    ppermute x1, waiting for transfers between devices, local(): got = lax.ppermute(give, 'c', swap)  5.65 us
    dynamic_update_slice x2, local copies, waits for them, and re-layouts, place(): return lax.dynamic_update_slice(pack, dmix, (1296, 0))  5.13 us
  transfers between devices with their start and end apart: 13, of which 1 were waited for; matrix products, arithmetic and copies ran while one was open for 8% of the time, Pallas kernels for 22%

commit v1 on v0

v1 whole, which is shorter than its diff:
```python
import functools

import jax
import jax.numpy as jnp
from jax import lax
from jax.experimental import pallas as pl
from jax.experimental.pallas import tpu as pltpu
from jax.sharding import Mesh, PartitionSpec as P

BF = jnp.bfloat16
F32 = jnp.float32
HIGH = lax.Precision.HIGHEST
LAT = ("y", "xl", "c")
ENS = ("z", "xh")
CHIPS = ("y", "xl", "z", "xh")
HALF = 48
CH = 96
HID = 512
COLS = 384
ROW = 768
CELLS = 1536
IN_ROWS = 448
IN_HALF = 224
TAP_HALF = 144
VMEM_LIMIT = 56 * 1024 * 1024


def mm(a, b):
    return lax.dot_general(a, b, (((1,), (0,)), ((), ())), preferred_element_type=F32)


def mm_nt(a, b):
    return lax.dot_general(a, b, (((1,), (1,)), ((), ())), preferred_element_type=F32)


def mm_high(a, b):
    return lax.dot_general(
        a, b, (((1,), (0,)), ((), ())), preferred_element_type=F32, precision=HIGH
    )


def split3(x):
    hi = x.astype(BF)
    rest = x - hi.astype(F32)
    mid = rest.astype(BF)
    low = (rest - mid.astype(F32)).astype(BF)
    return hi, mid, low


def from_left(x):
    lane = lax.broadcasted_iota(jnp.int32, x.shape, 1)
    return jnp.where(lane == 0, 0.0, pltpu.roll(x, 1, 1))


def from_right(x):
    width = x.shape[1]
    lane = lax.broadcasted_iota(jnp.int32, x.shape, 1)
    return jnp.where(lane == width - 1, 0.0, pltpu.roll(x, width - 1, 1))


def sds(shape, dtype):
    return jax.ShapeDtypeStruct(shape, dtype)


def call(body, outs, ins, scratch=(), smem=(), flops=0, name=None):
    moved = sum(x.size * x.dtype.itemsize for x in list(ins) + list(outs))
    return pl.pallas_call(
        body,
        out_shape=outs,
        in_specs=[
            pl.BlockSpec(memory_space=pltpu.SMEM if i in smem else pltpu.VMEM)
            for i in range(len(ins))
        ],
        out_specs=[pl.BlockSpec(memory_space=pltpu.VMEM) for _ in outs],
        scratch_shapes=list(scratch),
        compiler_params=pltpu.CompilerParams(vmem_limit_bytes=VMEM_LIMIT),
        cost_estimate=pl.CostEstimate(flops=flops, bytes_accessed=moved, transcendentals=0),
        name=name,
    )(*ins)


def payload_kernel(on_ref, grad_ref, out_ref):
    bands, width = on_ref.shape[2], 2 * CH
    blank = jnp.zeros(on_ref.shape[1:], BF)
    for s in range(on_ref.shape[0]):
        on = on_ref[s]
        hi = on.astype(BF)
        grad = grad_ref[s]
        ghi = grad.astype(BF)
        out_ref[s, :, :width] = hi
        out_ref[s, :, width : 2 * width] = (on - hi.astype(F32)).astype(BF)
        if s + 1 < on_ref.shape[0]:
            out_ref[s + 1, :, 2 * width : 3 * width] = hi
        if s > 0:
            out_ref[s - 1, :, 3 * width : 4 * width] = hi
        out_ref[s, :, 4 * width : 5 * width] = ghi
        out_ref[s, :, 5 * width : 6 * width] = (grad - ghi.astype(F32)).astype(BF)
    out_ref[0, :, 2 * width : 3 * width] = blank
    out_ref[on_ref.shape[0] - 1, :, 3 * width : 4 * width] = blank


def payload(on, grad):
    bands, width, channels = on.shape
    return call(
        payload_kernel, [sds((bands, width, 6 * channels), BF)], [on, grad], name="payload"
    )[0]


def prep_kernel(
    mix_ref, w1_ref, w2_ref, b1_ref, b2_ref, *refs
):
    stage1, stage2 = refs[-2:]
    flows = mix_ref.shape[0]
    row = lax.broadcasted_iota(jnp.int32, (CH, CH), 0)
    col = lax.broadcasted_iota(jnp.int32, (CH, CH), 1)
    eye = (row == col).astype(F32)
    near = (row // 16) == (col // 16)
    units = []
    for k in range(flows):
        mix = mix_ref[k]
        units.append(jnp.where(row > col, mix, 0.0))
        units.append(jnp.where(row < col, mix, 0.0))
    inner = [jnp.where(near, u, 0.0) for u in units]
    outer = [u - i for u, i in zip(units, inner)]
    power = inner
    blocks = [eye - n for n in inner]
    for _ in range(3):
        power = [mm_high(p, p) for p in power]
        blocks = [mm_high(b, eye + p) for b, p in zip(blocks, power)]
    power = [mm_high(b, o) for b, o in zip(blocks, outer)]
    whole = [eye - p for p in power]
    for _ in range(2):
        power = [mm_high(p, p) for p in power]
        whole = [mm_high(w, eye + p) for w, p in zip(whole, power)]
    inverses = [mm_high(w, b) for w, b in zip(whole, blocks)]
    for k in range(flows):
        inv_ref, lut_ref, w1t_ref, w2t_ref, w2k_ref, b2c_ref = refs[6 * k : 6 * k + 6]
        inv_ref[...] = mm_high(inverses[2 * k + 1], inverses[2 * k])
        lut_ref[...] = mm_high(units[2 * k] + eye, units[2 * k + 1] + eye).T
        for tap in range(9):
            stage1[tap * HALF : (tap + 1) * HALF, :] = 0.5 * w1_ref[k, tap].astype(F32)
            stage2[tap * CH : (tap + 1) * CH, :] = 0.5 * w2_ref[k, 8 - tap].astype(F32)
        hi, mid, low = split3(0.5 * b1_ref[k : k + 1, :])
        stage1[9 * HALF :, :] = jnp.zeros((IN_ROWS - 9 * HALF, HID), F32)
        for i, part in enumerate((hi, mid, low)):
            stage1[9 * HALF + i : 9 * HALF + i + 1, :] = part.astype(F32)
        w1t_ref[...] = stage1[...].T.astype(BF)
        w2t_ref[...] = stage2[...].T.astype(BF)
        for a in range(3):
            for b in range(3):
                w2k_ref[b * CH : (b + 1) * CH, a * HID : (a + 1) * HID] = w2_ref[k, 3 * a + b]
        b2c_ref[...] = jnp.broadcast_to(b2_ref[k : k + 1, :], (8, CH)).T


def prep(mix_factors, in_kernel, out_kernel, in_bias, out_bias):
    flows = mix_factors.shape[0]
    outs = call(
        prep_kernel,
        [
            sds((CH, CH), F32),
            sds((CH, CH), F32),
            sds((HID, IN_ROWS), BF),
            sds((HID, 9 * CH), BF),
            sds((3 * CH, 3 * HID), BF),
            sds((CH, 8), F32),
        ]
        * flows,
        [mix_factors, in_kernel, out_kernel, in_bias, out_bias],
        scratch=[pltpu.VMEM((IN_ROWS, HID), F32), pltpu.VMEM((9 * CH, HID), F32)],
        name="prep",
    )
    return [outs[i::6] for i in range(6)]


def turn_kernel(recv_ref, above_ref, mid_ref, below_ref, ya_ref, ga_ref, stage):
    width = 2 * CH
    row = lax.broadcasted_iota(jnp.int32, (width, width), 0)
    col = lax.broadcasted_iota(jnp.int32, (width, width), 1)
    pick = (col == 4 * (row % HALF) + row // HALF).astype(BF)
    none = jnp.zeros((width, width), BF)
    first = jnp.concatenate([pick, none], axis=1)
    second = jnp.concatenate([none, pick], axis=1)
    both = jnp.concatenate([pick, pick], axis=1)
    sources, count = recv_ref.shape[0], recv_ref.shape[1]
    for s in range(sources):
        stage[s * count : (s + 1) * count, :] = recv_ref[s].astype(F32)
    pair = stage[:, : 2 * width].astype(BF)
    kept = mm_nt(both, pair)
    mid_ref[...] = mm_nt(first, pair).astype(BF)
    pair = stage[:, 2 * width : 4 * width].astype(BF)
    above_ref[...] = mm_nt(first, pair).astype(BF)
    below_ref[...] = mm_nt(second, pair).astype(BF)
    grad = mm_nt(both, stage[:, 4 * width :].astype(BF))
    for k in range(4):
        ya_ref[:, k * COLS : (k + 1) * COLS] = kept[k * HALF : (k + 1) * HALF]
        ga_ref[:, k * COLS : (k + 1) * COLS] = grad[k * HALF : (k + 1) * HALF]


def turn(recv):
    return call(
        turn_kernel,
        [sds((2 * CH, COLS), BF)] * 3 + [sds((HALF, CELLS), F32)] * 2,
        [recv],
        scratch=[pltpu.VMEM((COLS, recv.shape[2]), F32)],
        name="turn",
    )


def stack_planes(even, odd, factor=None):
    if factor is not None:
        even = (even.astype(F32) * factor).astype(BF)
        odd = (odd.astype(F32) * factor).astype(BF)
    left = from_left(odd.astype(F32)).astype(BF)
    right = from_right(even.astype(F32)).astype(BF)
    return jnp.concatenate([left, even, odd, right], axis=0)


def fill_input_columns(flags_ref, above_ref, mid_ref, below_ref, columns, first, count):
    refs = {-2: (above_ref, 0), -1: (above_ref, CH), 0: (mid_ref, 0)}
    refs.update({1: (mid_ref, CH), 2: (below_ref, 0), 3: (below_ref, CH)})
    for source in range(first - 1, first + count + 1):
        ref, at = refs[source]
        factor = flags_ref[0] if source < 0 else flags_ref[1] if source > 1 else None
        stacked = stack_planes(ref[at : at + HALF], ref[at + HALF : at + CH], factor)
        for a in range(3):
            target = source - a + 1 - first
            if 0 <= target < count:
                for p in range(2):
                    lane = (2 * target + p) * COLS
                    columns[a * 144 : (a + 1) * 144, lane : lane + COLS] = stacked[
                        p * HALF : p * HALF + 144
                    ]
    extra = IN_ROWS - 9 * HALF
    row = lax.broadcasted_iota(jnp.int32, (extra, count * ROW), 0)
    columns[9 * HALF :, :] = jnp.where(row < 3, 1.0, 0.0).astype(BF)


def fill_grad_columns(flags_ref, top_ref, mid_ref, bottom_ref, columns):
    refs = [(top_ref, 0), (mid_ref, 0), (mid_ref, 2 * CH), (bottom_ref, 0)]
    for source in range(4):
        ref, at = refs[source]
        factor = flags_ref[0] if source == 0 else flags_ref[1] if source == 3 else None
        stacked = stack_planes(ref[at : at + CH], ref[at + CH : at + 2 * CH], factor)
        for a in range(3):
            target = source - a
            if 0 <= target < 2:
                for p in range(2):
                    lane = (2 * target + p) * COLS
                    columns[a * 288 : (a + 1) * 288, lane : lane + COLS] = stacked[
                        p * CH : p * CH + 288
                    ]


def put_out_grad(raw, moved, out_ref):
    for r in range(2):
        for p in range(2):
            lane = (2 * r + p) * COLS
            at = (2 * r + p) * CH
            out_ref[at : at + HALF] = raw[:, lane : lane + COLS].astype(BF)
            out_ref[at + HALF : at + CH] = moved[:, lane : lane + COLS].astype(BF)


def forward_kernel(with_grad, flags_ref, *refs):
    above_ref, mid_ref, below_ref, w1t_ref, w2k_ref, b2_ref, inv_ref, ya_ref, yb_ref = refs[:9]
    columns, pre, outs = refs[-3:]
    if with_grad:
        x_ref, rows, slope_ref, next_ref, grad_ref, moved_ref, up_ref, down_ref = refs[9:-3]
    else:
        x_ref, rows, slope_ref, scale_ref = refs[9:-3]
    fill_input_columns(flags_ref, above_ref, mid_ref, below_ref, columns, -1, 4)
    for h in range(4):
        pre[h % 2] = mm(w1t_ref[...], columns[:, h * ROW : (h + 1) * ROW])
        inside = flags_ref[0] if h == 0 else flags_ref[1] if h == 3 else None

        def activate(step, carry):
            at = pl.multiple_of(step * 16, 16)
            half = pre[h % 2, pl.ds(at, 16), :]
            bent = jnp.tanh(half)
            more = 1.0 + bent
            hidden = half * more
            if inside is not None:
                rows[pl.ds(h * HID + at, 16), :] = (hidden * inside).astype(BF)
            else:
                rows[pl.ds(h * HID + at, 16), :] = hidden.astype(BF)
                slope_ref[pl.ds((h - 1) * HID + at, 16), :] = more * (1.0 + half * (1.0 - bent))
            return carry

        lax.fori_loop(0, HID // 16, activate, 0, unroll=UNROLL)
    for r in range(2):
        taps = mm(w2k_ref[...], rows[r * HID : (r + 3) * HID, :])
        even, odd = taps[:, :COLS], taps[:, COLS:]
        lane = 2 * r * COLS
        outs[:, lane : lane + COLS] = from_left(odd[:CH]) + even[CH : 2 * CH] + odd[2 * CH :]
        outs[:, lane + COLS : lane + ROW] = even[:CH] + odd[CH : 2 * CH] + from_right(even[2 * CH :])
    raw = outs[:HALF] + b2_ref[:HALF, :1]
    shift = outs[HALF:] + b2_ref[HALF:, :1]
    inverse = 1.0 + jnp.exp(-(raw + 2.0))
    scale = 1.0 / inverse
    moved_in = yb_ref[...] * inverse - shift
    x = mm_high(inv_ref[...], jnp.concatenate([ya_ref[...], moved_in], axis=0))
    x_ref[...] = x
    if with_grad:
        moved_grad = yb_ref[...]
        moved = moved_grad * scale
        moved_ref[...] = moved
        put_out_grad((moved_grad * yb_ref[...] - 1.0) * (1.0 - scale), moved, grad_ref)
        for k in range(4):
            next_ref[k * HALF : (k + 1) * HALF] = x[:HALF, k * COLS : (k + 1) * COLS].astype(BF)
        up_ref[: 2 * CH] = grad_ref[: 2 * CH]
        down_ref[: 2 * CH] = grad_ref[2 * CH :]
        up_ref[2 * CH :] = next_ref[...]
        down_ref[2 * CH :] = next_ref[...]
    else:
        scale_ref[...] = scale


UNROLL = 4


def forward(flags, above, mid, below, w1t, w2k, b2c, inv, ya, yb, with_grad):
    outs = [sds((CH, CELLS), F32), sds((4 * HID, ROW), BF), sds((2 * HID, ROW), F32)]
    if with_grad:
        outs += [
            sds((2 * CH, COLS), BF),
            sds((4 * CH, COLS), BF),
            sds((HALF, CELLS), F32),
            sds((4 * CH, COLS), BF),
            sds((4 * CH, COLS), BF),
        ]
    else:
        outs += [sds((HALF, CELLS), F32)]
    return call(
        functools.partial(forward_kernel, with_grad),
        outs,
        [flags, above, mid, below, w1t, w2k, b2c, inv, ya, yb],
        scratch=[
            pltpu.VMEM((IN_ROWS, 4 * ROW), BF),
            pltpu.VMEM((2, HID, ROW), F32),
            pltpu.VMEM((CH, CELLS), F32),
        ],
        smem=(0,),
        flops=4 * 10**9,
        name="forward",
    )


def backward_kernel(
    flow, flags_ref, top_ref, mid_ref, bottom_ref, w2t_ref, slope_ref, w1_ref, gpre_ref, up_ref, in_ref,
    down_ref, columns, hid_grad, sums,
):
    fill_grad_columns(flags_ref, top_ref, mid_ref, bottom_ref, columns)
    sums[0] = jnp.zeros_like(sums[0])
    for r in range(2):
        hid_grad[r] = mm(w2t_ref[...], columns[:, r * ROW : (r + 1) * ROW])

        def slope(step, carry):
            at = pl.multiple_of(step * 16, 16)
            gpre_ref[pl.ds(r * HID + at, 16), :] = (
                hid_grad[r, pl.ds(at, 16), :] * slope_ref[pl.ds(r * HID + at, 16), :]
            ).astype(BF)
            return carry

        lax.fori_loop(0, HID // 16, slope, 0, unroll=UNROLL)
        taps = mm(w1_ref[flow], gpre_ref[r * HID : (r + 1) * HID, :])
        for a in range(3):
            part = taps[a * 144 : (a + 1) * 144]
            if r == 0 or a == 2:
                sums[r + a] = part
            else:
                sums[r + a] += part
    for row, (ref, at) in enumerate(((up_ref, 0), (in_ref, 0), (in_ref, CH), (down_ref, 0))):
        total = sums[row]
        even, odd = total[:, :COLS], total[:, COLS:]
        b0, b1, b2 = slice(0, HALF), slice(HALF, CH), slice(CH, 3 * HALF)
        new_even = odd[b0] + even[b1] + from_left(odd[b2])
        new_odd = from_right(even[b0]) + odd[b1] + even[b2]
        ref[at : at + HALF] = new_even.astype(ref.dtype)
        ref[at + HALF : at + CH] = new_odd.astype(ref.dtype)


def backward(flags, top, mid, bottom, w2t, slope, w1, flow):
    return call(
        functools.partial(backward_kernel, flow),
        [
            sds((2 * HID, ROW), BF),
            sds((CH, COLS), BF),
            sds((2 * CH, COLS), F32),
            sds((CH, COLS), BF),
        ],
        [flags, top, mid, bottom, w2t, slope, w1],
        scratch=[
            pltpu.VMEM((9 * CH, CELLS), BF),
            pltpu.VMEM((2, HID, ROW), F32),
            pltpu.VMEM((4, 144, ROW), F32),
        ],
        smem=(0,),
        flops=4 * 10**9,
        name="backward",
    )


def out_weight_kernel(core_ref, grad_ref, rows_ref, keep_ref, give_ref, bias_ref, left, right):
    for r in range(2):
        at = 2 * r * CH
        stacked = stack_planes(grad_ref[at : at + CH], grad_ref[at + CH : at + 2 * CH])
        left[r] = stacked[: 3 * CH]
        right[r] = stacked[CH:]
    for ref, core in ((keep_ref, core_ref[0]), (give_ref, 1 - core_ref[0])):
        at = pl.multiple_of(core * TAP_HALF, 16)
        part = [
            jnp.concatenate(
                [left[r, pl.ds(at, TAP_HALF), :], right[r, pl.ds(at, TAP_HALF), :]], axis=1
            )
            for r in range(2)
        ]
        for a in range(3):
            ref[a] = mm_nt(part[0], rows_ref[a * HID : (a + 1) * HID]) + mm_nt(
                part[1], rows_ref[(a + 1) * HID : (a + 2) * HID]
            )
    ones = jnp.ones((8, COLS), BF)
    total = mm_nt(ones, grad_ref[:CH]) + mm_nt(ones, grad_ref[CH : 2 * CH])
    bias_ref[...] = total + (
        mm_nt(ones, grad_ref[2 * CH : 3 * CH]) + mm_nt(ones, grad_ref[3 * CH :])
    )


def out_weight(core, grad, rows):
    return call(
        out_weight_kernel,
        [sds((3, TAP_HALF, HID), F32), sds((3, TAP_HALF, HID), F32), sds((8, CH), F32)],
        [core, grad, rows],
        scratch=[pltpu.VMEM((2, 3 * CH, COLS), BF), pltpu.VMEM((2, 3 * CH, COLS), BF)],
        smem=(0,),
        flops=2 * 10**9,
        name="out_weight",
    )


def in_weight_kernel(
    core_ref, flags_ref, above_ref, mid_ref, below_ref, gpre_ref, keep_ref, give_ref, columns
):
    fill_input_columns(flags_ref, above_ref, mid_ref, below_ref, columns, 0, 2)
    for ref, core in ((keep_ref, core_ref[0]), (give_ref, 1 - core_ref[0])):
        at = pl.multiple_of(core * IN_HALF, 16)
        part = columns[pl.ds(at, IN_HALF), :]
        ref[...] = mm_nt(part[:, :ROW], gpre_ref[:HID]) + mm_nt(part[:, ROW:], gpre_ref[HID:])


def in_weight(core, flags, above, mid, below, gpre):
    return call(
        in_weight_kernel,
        [sds((IN_HALF, HID), F32), sds((IN_HALF, HID), F32)],
        [core, flags, above, mid, below, gpre],
        scratch=[pltpu.VMEM((IN_ROWS, CELLS), BF)],
        smem=(0, 1),
        flops=10**9,
        name="in_weight",
    )


def close_kernel(next_step, flow, core_ref, flags_ref, *refs):
    in_ref, low_ref, high_ref, ga_ref, moved_ref, lut_ref, x_ref, mix_ref, bias_ref = refs[:9]
    whole, small = refs[-2:]
    if next_step:
        scale_ref, gx_ref, keep_ref, give_ref, grad_ref, nmoved_ref = refs[9:-2]
    else:
        gx_ref, keep_ref, give_ref = refs[9:-2]
    for k in range(4):
        part = in_ref[k * HALF : (k + 1) * HALF]
        if k < 2:
            part = part + flags_ref[0] * low_ref[k * HALF : (k + 1) * HALF].astype(F32)
        else:
            part = part + flags_ref[1] * high_ref[(k - 2) * HALF : (k - 1) * HALF].astype(F32)
        lane = k * COLS
        whole[:HALF, lane : lane + COLS] = ga_ref[:HALF, lane : lane + COLS] + part
    whole[HALF:] = moved_ref[...]
    gx = mm_high(lut_ref[...], whole[...])
    gx_ref[...] = gx
    if next_step:
        scale = scale_ref[...]
        moved_grad = gx[HALF:]
        moved = moved_grad * scale
        nmoved_ref[...] = moved
        put_out_grad((moved_grad * x_ref[HALF:] - 1.0) * (1.0 - scale), moved, grad_ref)
    ghi, gmid, _ = split3(whole[...])
    xhi, xmid, _ = split3(x_ref[...])
    outer = mm_nt(ghi, xhi) + (mm_nt(ghi, xmid) + mm_nt(gmid, xhi))
    row = lax.broadcasted_iota(jnp.int32, (CH, CH), 0)
    col = lax.broadcasted_iota(jnp.int32, (CH, CH), 1)
    eye = (row == col).astype(F32)
    mix = mix_ref[flow]
    lower = jnp.where(row > col, mix, 0.0) + eye
    upper = jnp.where(row < col, mix, 0.0) + eye
    by_upper = mm_high(outer, upper.T)
    by_lower = mm_high(lower.T, outer)
    small[:, :CH] = jnp.where(row > col, by_upper, jnp.where(row < col, by_lower, 0.0))
    small[:, CH:] = jnp.zeros((CH, 2 * 128 - CH), F32)
    small[:8, 128 : 128 + CH] = bias_ref[...]
    for ref, core in ((keep_ref, core_ref[0]), (give_ref, 1 - core_ref[0])):
        ref[...] = small[pl.ds(pl.multiple_of(core * HALF, 8), HALF), :]


def close(core, flags, gin, low, high, ga, moved, lut, x, mix, flow, bias, scale=None):
    outs = [sds((CH, CELLS), F32), sds((HALF, 256), F32), sds((HALF, 256), F32)]
    ins = [core, flags, gin, low, high, ga, moved, lut, x, mix, bias]
    if scale is not None:
        outs += [sds((4 * CH, COLS), BF), sds((HALF, CELLS), F32)]
        ins += [scale]
    return call(
        functools.partial(close_kernel, scale is not None, flow),
        outs,
        ins,
        scratch=[pltpu.VMEM((CH, CELLS), F32), pltpu.VMEM((CH, 256), F32)],
        smem=(0, 1),
        flops=10**9,
        name="close",
    )


def weave_kernel(x_ref, out_ref):
    size = 256
    row = lax.broadcasted_iota(jnp.int32, (size, size), 0)
    col = lax.broadcasted_iota(jnp.int32, (size, size), 1)
    place = (col == 2 * (row % 128) + row // 128).astype(BF)
    for r in range(2):
        for t in range(3):
            lane = r * ROW + t * 128
            pair = jnp.concatenate(
                [x_ref[:, lane : lane + 128], x_ref[:, lane + COLS : lane + COLS + 128]], axis=1
            )
            hi, mid, low = split3(pair)
            woven = mm(hi, place) + (mm(mid, place) + mm(low, place))
            out_ref[0, :, r, t * size : (t + 1) * size] = woven


def weave(x):
    return call(weave_kernel, [sds((1, CH, 2, ROW), F32)], [x], name="weave")[0]


PARTS = ((0, IN_HALF), (224, TAP_HALF), (368, TAP_HALF), (512, TAP_HALF), (656, HALF))
FLOW_ROWS = 704
GROUP = 88


def merge_kernel(*refs):
    out_ref, total = refs[-2:]
    for k in range(2):
        own_in, own_out, own_small, got_in, got_out, got_small = refs[6 * k : 6 * k + 6]
        at = k * FLOW_ROWS
        total[at : at + IN_HALF] = own_in[...] + got_in[...]
        for a in range(3):
            start = at + IN_HALF + a * TAP_HALF
            total[start : start + TAP_HALF] = own_out[a] + got_out[a]
        small = own_small[...] + got_small[...]
        start = at + FLOW_ROWS - HALF
        total[start : start + HALF, :256] = small
        total[start : start + HALF, 256:] = small - small.astype(BF).astype(F32)
    for g in range(2 * FLOW_ROWS // GROUP):
        for lane in range(4):
            out_ref[4 * g + lane] = total[
                g * GROUP : (g + 1) * GROUP, lane * 128 : (lane + 1) * 128
            ].astype(BF)


def merge(own0, got0, own1, got1):
    shares = 2 * FLOW_ROWS // GROUP * 4
    return call(
        merge_kernel,
        [sds((shares, GROUP, 128), BF)],
        [*own0, *got0, *own1, *got1],
        scratch=[pltpu.VMEM((2 * FLOW_ROWS, HID), F32)],
        name="merge",
    )[0]


def total_kernel(cells, shares_ref, out_ref):
    total = shares_ref[0].astype(F32)
    for s in range(1, shares_ref.shape[0]):
        total += shares_ref[s].astype(F32)
    mean = (total * (1.0 / cells)).astype(BF)
    for s in range(shares_ref.shape[0]):
        out_ref[s] = mean


def totals(shares, cells):
    return call(
        functools.partial(total_kernel, cells), [sds(shares.shape, BF)], [shares], name="totals"
    )[0]


def unpack_kernel(core_ref, mine_ref, other_ref, win_ref, wout_ref, mix_ref, bin_ref, bout_ref, rows):
    mine_first = core_ref[0] == 0
    for half in range(2):
        for g in range(2 * FLOW_ROWS // GROUP):
            for lane in range(4):
                mine = mine_ref[4 * g + lane].astype(F32)
                other = other_ref[4 * g + lane].astype(F32)
                first, second = (mine, other) if half == 0 else (other, mine)
                rows[half, g * GROUP : (g + 1) * GROUP, lane * 128 : (lane + 1) * 128] = jnp.where(
                    mine_first, first, second
                )
    for k in range(2):
        at = k * FLOW_ROWS
        win_ref[k, :IN_HALF] = rows[0, at : at + IN_HALF]
        win_ref[k, IN_HALF:] = rows[1, at : at + 9 * HALF - IN_HALF]
        bin_ref[k : k + 1, :] = rows[1, at + 9 * HALF - IN_HALF : at + 9 * HALF - IN_HALF + 1]
        for a in range(3):
            start = at + IN_HALF + a * TAP_HALF
            wout_ref[k, 3 * a + 2] = rows[0, start : start + CH]
            wout_ref[k, 3 * a + 1, :HALF] = rows[0, start + CH : start + TAP_HALF]
            wout_ref[k, 3 * a + 1, HALF:] = rows[1, start : start + HALF]
            wout_ref[k, 3 * a] = rows[1, start + HALF : start + TAP_HALF]
        start = at + FLOW_ROWS - HALF
        for half in range(2):
            block = rows[half, start : start + HALF]
            mix_ref[k, half * HALF : (half + 1) * HALF] = block[:, :CH] + block[:, 256 : 256 + CH]
        block = rows[0, start : start + 8]
        bout_ref[k] = block[:, 128 : 128 + CH] + block[:, 384 : 384 + CH]


def unpack(core, mine, other):
    return call(
        unpack_kernel,
        [
            sds((2, 9 * HALF, HID), F32),
            sds((2, 9, CH, HID), F32),
            sds((2, CH, CH), F32),
            sds((2, HID), F32),
            sds((2, 8, CH), F32),
        ],
        [core, mine, other],
        scratch=[pltpu.VMEM((2, 2 * FLOW_ROWS, HID), F32)],
        smem=(0,),
        name="unpack",
    )


def local(passed_on, passed_grad, latent, mix_factors, in_kernel, in_bias, out_kernel, out_bias):
    lat_index = lax.axis_index(LAT)
    lat_count = lax.axis_size(LAT)
    forth = [(i, (i + 1) % lat_count) for i in range(lat_count)]
    back = [(t, s) for s, t in forth]
    swap = [(0, 1), (1, 0)]
    flags = jnp.stack([lat_index > 0, lat_index < lat_count - 1]).astype(F32)
    core = lax.axis_index("c").astype(jnp.int32).reshape(1)

    block = payload(
        jnp.transpose(passed_on[0], (1, 2, 0)), jnp.transpose(passed_grad[0], (1, 2, 0))
    )
    recv = lax.all_to_all(block, LAT, 0, 0, tiled=True)
    inv, lut, w1t, w2t, w2k, b2c = prep(mix_factors, in_kernel, out_kernel, in_bias, out_bias)
    w1 = in_kernel.reshape(2, 9 * HALF, HID)
    yb = latent.reshape(HALF, CELLS)

    above, mid, below, ya, ga = turn(recv)
    x1, rows1, slope1, next_mid, grad1, moved1, up, down = forward(
        flags, above, mid, below, w1t[1], w2k[1], b2c[1], inv[1], ya, yb, True
    )
    from_above = lax.ppermute(down, LAT, forth)
    from_below = lax.ppermute(up, LAT, back)
    keep_out1, give_out1, bias1 = out_weight(core, grad1, rows1)
    top1, above0 = from_above[: 2 * CH], from_above[2 * CH :]
    bottom1, below0 = from_below[: 2 * CH], from_below[2 * CH :]
    gpre1, up1, in1, down1 = backward(flags, top1, grad1, bottom1, w2t[1], slope1, w1, 1)
    low1 = lax.ppermute(down1, LAT, forth)
    high1 = lax.ppermute(up1, LAT, back)
    got_out1 = lax.ppermute(give_out1, "c", swap)
    x0, rows0, slope0, scale0 = forward(
        flags, above0, next_mid, below0, w1t[0], w2k[0], b2c[0], inv[0],
        x1[:HALF], x1[HALF:], False,
    )
    gx1, keep_small1, give_small1, grad0, moved0 = close(
        core, flags, in1, low1, high1, ga, moved1, lut[1], x1, mix_factors, 1, bias1, scale0
    )
    top0 = lax.ppermute(grad0[2 * CH :], LAT, forth)
    bottom0 = lax.ppermute(grad0[: 2 * CH], LAT, back)
    keep_in1, give_in1 = in_weight(core, flags, above, mid, below, gpre1)
    keep_out0, give_out0, bias0 = out_weight(core, grad0, rows0)
    got_in1 = lax.ppermute(give_in1, "c", swap)
    got_small1 = lax.ppermute(give_small1, "c", swap)
    got_out0 = lax.ppermute(give_out0, "c", swap)
    gpre0, up0, in0, down0 = backward(flags, top0, grad0, bottom0, w2t[0], slope0, w1, 0)
    low0 = lax.ppermute(down0, LAT, forth)
    high0 = lax.ppermute(up0, LAT, back)
    keep_in0, give_in0 = in_weight(core, flags, above0, next_mid, below0, gpre0)
    got_in0 = lax.ppermute(give_in0, "c", swap)
    gx0, keep_small0, give_small0 = close(
        core, flags, in0, low0, high0, gx1, moved0, lut[0], x0, mix_factors, 0, bias0
    )
    got_small0 = lax.ppermute(give_small0, "c", swap)

    shares = lax.all_to_all(
        merge(
            (keep_in0, keep_out0, keep_small0),
            (got_in0, got_out0, got_small0),
            (keep_in1, keep_out1, keep_small1),
            (got_in1, got_out1, got_small1),
        ),
        CHIPS, 0, 0, tiled=True,
    )
    cells = float(CELLS * lat_count * lax.axis_size(ENS))
    mine = lax.all_to_all(totals(shares, cells), CHIPS, 0, 0, tiled=True)
    other = lax.ppermute(mine, "c", swap)
    rebuilt = weave(x0)
    input_grad = weave(gx0)
    in_grad, out_grad, mix_grad, in_bias_grad, out_bias_grad = unpack(core, mine, other)
    return (
        rebuilt,
        input_grad,
        mix_grad,
        in_grad.reshape(2, 9, HALF, HID),
        in_bias_grad,
        out_grad,
        out_bias_grad[:, 0],
    )


def solution(mesh):
    split = Mesh(mesh.devices.reshape(4, 2, 2, 4, 2), ("y", "xl", "c", "z", "xh"))
    return jax.shard_map(
        local,
        mesh=split,
        in_specs=(
            P(ENS, None, None, LAT),
            P(ENS, None, None, LAT),
            P(ENS, None, LAT, None),
            P(),
            P(),
            P(),
            P(),
            P(),
        ),
        out_specs=(P(ENS, None, LAT, None), P(ENS, None, LAT, None), P(), P(), P(), P(), P()),
        check_vma=False,
    )
```

time: 251 us -> 201 us (0.80)
  local copies, waits for them, and re-layouts: 33.5 us -> 11.3 us
  starting transfers between devices: 41.5 us -> 28.2 us
  other arithmetic: 10.3 us -> 1.27 us
  blocking collectives: 63.6 us -> 57.4 us
  waiting for transfers between devices: 5.68 us -> 8.31 us
    squeeze x11 -> x0, local copies, waits for them, and re-layouts: 9.58 us -> none  [the longest x1 2.4 us: local(): w1t[0]]
    all_to_all x2, blocking collectives: 63.6 us -> 57.4 us  [the longest x1 32.6 us: local(): lax.all_to_all(merge((keep_in0, keep_out0, keep_small0), (got_in0, got_ou...]
    dynamic_update_slice x2 -> x0, local copies, waits for them, and re-layouts: 5.13 us -> none  [place(): return lax.dynamic_update_slice(pack, dmix, (1296, 0))]
    ppermute x7 -> x10, starting transfers between devices: 17.2 us -> 12.2 us  [the longest x1 3.53 us: local(): got_out1 = lax.ppermute(give_out1, 'c', swap)]
    all_to_all x1, waiting for transfers between devices: 0.01 us -> 4.87 us  [local(): recv = lax.all_to_all(block, LAT, 0, 0, tiled=True)]
    ppermute x1, starting transfers between devices: 4.64 us -> 0.01 us  [local(): low0 = lax.ppermute(down0, LAT, forth)]
    ppermute x7 -> x10, waiting for transfers between devices: 5.66 us -> 1.12 us  [the longest x1 1.09 us: local(): got_small0 = lax.ppermute(give_small0, 'c', swap)]
    ppermute x1, starting transfers between devices: 4.26 us -> 0.01 us  [local(): low1 = lax.ppermute(down1, LAT, forth)]
  transfers between devices with their start and end apart: 13 -> 16, of which waited for: 1 -> 4; matrix products, arithmetic and copies ran while one was open for 8% -> 3% of each run, Pallas kernels for 22% -> 32%
where the time goes in v1:
time: 201 us; the launch traced here: 200 us
  Pallas kernels  92.6 us (46%)
  blocking collectives  57.4 us (29%)
  starting transfers between devices  28.2 us (14%)
  local copies, waits for them, and re-layouts  11.3 us (6%)
  waiting for transfers between devices  8.31 us (4%)
    pallas_call x18, Pallas kernels, call(): pl.pallas_call(body, out_shape=outs, in_specs=[pl.BlockSpec(memory_space=...  92.6 us
    all_to_all x1, blocking collectives, local(): lax.all_to_all(merge((keep_in0, keep_out0, keep_small0), (got_in0, got_ou...  32.6 us
    all_to_all x1, blocking collectives, local(): mine = lax.all_to_all(totals(shares, cells), CHIPS, 0, 0, tiled=True)  24.8 us
    all_to_all x1, starting transfers between devices, local(): recv = lax.all_to_all(block, LAT, 0, 0, tiled=True)  6.91 us
    all_to_all x1, waiting for transfers between devices, local(): recv = lax.all_to_all(block, LAT, 0, 0, tiled=True)  4.87 us
    unnamed x38, local copies, waits for them, and re-layouts  4.85 us
    ppermute x1, starting transfers between devices, local(): high0 = lax.ppermute(up0, LAT, back)  4.55 us
    ppermute x1, starting transfers between devices, local(): other = lax.ppermute(mine, 'c', swap)  4.02 us
  transfers between devices with their start and end apart: 16, of which 4 were waited for; matrix products, arithmetic and copies ran while one was open for 3% of the time, Pallas kernels for 32%

profile of v1, /device:TPU:1, one launch (start us, length us, event | category | flops | bytes accessed | tf_op | source)
XLA Modules:
  0.0 199.9 jit_solution(12088702873289905041)
XLA Ops:
  0.6 2.3 %payload.1 = bf16[16,24,1152]{2,1,0:T(8,128)(2,1)} custom-call(f32[16,24,192]{2,1,0:T(8,128)} %bitcast.14, f32[16,24,192]{2,1,0:T(8,128)} %bitcast.15), custom_call_target="tpu_custom_call" | custom-call | bytes 1474560 | tf_op jit(solution)/shard_map/payload/pallas_call | solution.py:67
  2.9 6.9 %all-to-all-start = ((bf16[16,24,1152]{2,1,0:T(8,128)(2,1)}), bf16[16,24,1152]{2,1,0:T(8,128)(2,1)S(1)}, u32[]{:S(2)}, u32[]{:S(2)}) async-start(bf16[16,24,1152]{2,1,0:T(8,128)(2,1)} %payload.1), calls=%async_computation | async-start | bytes 1769472 | tf_op jit(solution)/shard_map/all_to_all | solution.py:650
  11.3 7.1 %prep.1 = (f32[96,96]{1,0:T(8,128)}, f32[96,96]{1,0:T(8,128)}, bf16[512,448]{1,0:T(8,128)(2,1)}, bf16[512,864]{1,0:T(8,128)(2,1)}, bf16[288,1536]{1,0:T(8,128)(2...) custom-call(f32[2,96,96]{2,1,0:T(8,128)} %refs_7_.3, ...), custom_call_target="tpu_custom_call" | custom-call | bytes 7342848 | tf_op jit(solution)/shard_map/prep/pallas_call | solution.py:67
  19.0 4.9 %all-to-all-done.recv_ref = bf16[16,24,1152]{2,1,0:T(8,128)(2,1)S(1)} async-done(((bf16[16,24,1152]{2,1,0:T(8,128)(2,1)}), bf16[16,24,1152]{2,1,0:T(8,128)(2,1)S(1)}, u32[]{:S(2)}, u32[]{:S(2)}) %all-to-all-start) | async-done | bytes 884768 | tf_op jit(solution)/shard_map/all_to_all | solution.py:650
  24.8 2.6 %turn.1 = (bf16[192,384]{1,0:T(8,128)(2,1)}, bf16[192,384]{1,0:T(8,128)(2,1)}, bf16[192,384]{1,0:T(8,128)(2,1)}, f32[48,1536]{1,0:T(8,128)}, f32[48,1536]{1,0:T(8,128)}) custom-call(bf16[16,24,1152]{2,1,0:T(8,128)(2,1)} %copy-done.1), custom_call_target="tpu_custom_call" | custom-call | bytes 1916928 | tf_op jit(solution)/shard_map/turn/pallas_call | solution.py:67
  27.4 11.2 %forward.2 = (f32[96,1536]{1,0:T(8,128)}, bf16[2048,768]{1,0:T(8,128)(2,1)}, f32[1024,768]{1,0:T(8,128)}, bf16[192,384]{1,0:T(8,128)(2,1)}, bf16[384,384]{1,0:T(...) custom-call(f32[2]{0:T(128)} %add_convert_fusion.flags_ref, ...), custom_call_target="tpu_custom_call" | custom-call | flops 4000000000 | bytes 10624008 | tf_op jit(solution)/shard_map/forward/pallas_call | solution.py:67
  38.7 1.3 collective-permute-start
  39.9 1.9 fusion
  41.8 6.4 %out_weight.2 = (f32[3,144,512]{2,1,0:T(8,128)}, f32[3,144,512]{2,1,0:T(8,128)}, f32[8,96]{1,0:T(8,128)}) custom-call(s32[1]{0:T(128)} %bitcast.6.core_ref, bf16[384,384]{1,0:T(8,128)(2,1)} %get-tuple-element.84.mid_ref.grad_ref, bf16[2048,768]{1,0:T(8,128)(2,1)} %get-tuple-element.93.rows_ref), custom_call_target="tpu_custom_call" | custom-call | flops 2000000000 | bytes 5213188 | tf_op jit(solution)/shard_map/out_weight/pallas_call | solution.py:67
  48.2 3.5 %collective-permute-start.12 = (f32[3,144,512]{2,1,0:T(8,128)}, f32[3,144,512]{2,1,0:T(8,128)S(1)}, u32[]{:S(2)}, u32[]{:S(2)}) collective-permute-start(f32[3,144,512]{2,1,0:T(8,128)} %get-tuple-element.120), channel_id=1, source_target_pairs={{0,8},{8,0},{1,9},{9,1},{2,10},{10,2},{3,11},{11,3},{4,12},{12,4},... | collective-permute-start | bytes 2654216 | tf_op jit(solution)/shard_map/ppermute | solution.py:667
  53.2 7.5 %backward.2 = (bf16[1024,768]{1,0:T(8,128)(2,1)}, bf16[96,384]{1,0:T(8,128)(2,1)}, f32[192,384]{1,0:T(8,128)}, bf16[96,384]{1,0:T(8,128)(2,1)}) custom-call(f32[2]{0:T(128)} %add_convert_fusion.flags_ref, bf16[192,384]{1,0:T(8,128)(2,1)} %get-tuple-element.133.top_ref, bf16[384,384]{1,0:T(8,128)(2,1)} %get-tuple-element.84.mid_ref.grad_ref, ...), custom_call_target="tpu_custom_call" | custom-call | flops 4000000000 | bytes 7520264 | tf_op jit(solution)/shard_map/backward/pallas_call | solution.py:67
  61.3 3.7 %in_weight.3 = (f32[224,512]{1,0:T(8,128)}, f32[224,512]{1,0:T(8,128)}) custom-call(s32[1]{0:T(128)} %bitcast.6.core_ref, f32[2]{0:T(128)} %add_convert_fusion.flags_ref, bf16[192,384]{1,0:T(8,128)(2,1)} %get-tuple-element.67.refs_0_.above_ref, bf16[192,384]{1,0:T(8,128)(2,1)} %get-tuple-element.68.refs_1_.mid_ref, ...), custom_call_target="tpu_custom_call" | custom-call | flops 1000000000 | bytes 2932748 | tf_op jit(solution)/shard_map/in_weight/pallas_call | solution.py:67
  65.0 3.4 %collective-permute-start.11 = (f32[224,512]{1,0:T(8,128)}, f32[224,512]{1,0:T(8,128)S(1)}, u32[]{:S(2)}, u32[]{:S(2)}) collective-permute-start(f32[224,512]{1,0:T(8,128)} %get-tuple-element.119), channel_id=1, source_target_pairs={{0,8},{8,0},{1,9},{9,1},{2,10},{10,2},{3,11},{11,3},{4,12},{12,4},... | collective-permute-start | bytes 1376264 | tf_op jit(solution)/shard_map/ppermute | solution.py:679
  68.3 10.9 %forward.3 = (f32[96,1536]{1,0:T(8,128)}, bf16[2048,768]{1,0:T(8,128)(2,1)}, f32[1024,768]{1,0:T(8,128)}, f32[48,1536]{1,0:T(8,128)}) custom-call(f32[2]{0:T(128)} %add_convert_fusion.flags_ref, bf16[192,384]{1,0:T(8,128)(2,1)} %get-tuple-element.134.refs_0_.above_ref, bf16[192,384]{1,0:T(8,128)(2,1)} %get-tuple-element.76.refs_1_.mid_ref, ...), custom_call_target="tpu_custom_call" | custom-call | flops 4000000000 | bytes 9591816 | tf_op jit(solution)/shard_map/forward/pallas_call | solution.py:67
  79.9 3.5 %close.2 = (f32[96,1536]{1,0:T(8,128)}, f32[48,256]{1,0:T(8,128)}, f32[48,256]{1,0:T(8,128)}, bf16[384,384]{1,0:T(8,128)(2,1)}, f32[48,1536]{1,0:T(8,128)}) custom-call(s32[1]{0:T(128)} %bitcast.6.core_ref, f32[2]{0:T(128)} %add_convert_fusion.flags_ref, f32[192,384]{1,0:T(8,128)} %get-tuple-element.87.refs_0_, bf16[96,384]{1,0:T(8,128)(2,1)} %copy-done.12, ...), custom_call_target="tpu_custom_call" | custom-call | flops 1000000000 | bytes 3308556 | tf_op jit(solution)/shard_map/close/pallas_call | solution.py:67
  84.4 1.7 collective-permute-start.4
  86.2 6.3 %out_weight.3 = (f32[3,144,512]{2,1,0:T(8,128)}, f32[3,144,512]{2,1,0:T(8,128)}, f32[8,96]{1,0:T(8,128)}) custom-call(s32[1]{0:T(128)} %bitcast.6.core_ref, bf16[384,384]{1,0:T(8,128)(2,1)} %get-tuple-element.96.mid_ref.grad_ref, bf16[2048,768]{1,0:T(8,128)(2,1)} %get-tuple-element.105.rows_ref), custom_call_target="tpu_custom_call" | custom-call | flops 2000000000 | bytes 5213188 | tf_op jit(solution)/shard_map/out_weight/pallas_call | solution.py:67
  93.2 7.5 %backward.3 = (bf16[1024,768]{1,0:T(8,128)(2,1)}, bf16[96,384]{1,0:T(8,128)(2,1)}, f32[192,384]{1,0:T(8,128)}, bf16[96,384]{1,0:T(8,128)(2,1)}) custom-call(f32[2]{0:T(128)} %add_convert_fusion.flags_ref, bf16[192,384]{1,0:T(8,128)(2,1)} %copy-done.11, bf16[384,384]{1,0:T(8,128)(2,1)} %get-tuple-element.96.mid_ref.grad_ref, bf16[192,384]{1,0:T(8,128)(2,1)} %copy-done.10, ...), custom_call_target="tpu_custom_call" | custom-call | flops 4000000000 | bytes 7520264 | tf_op jit(solution)/shard_map/backward/pallas_call | solution.py:67
  100.7 3.7 %in_weight.2 = (f32[224,512]{1,0:T(8,128)}, f32[224,512]{1,0:T(8,128)}) custom-call(s32[1]{0:T(128)} %bitcast.6.core_ref, f32[2]{0:T(128)} %add_convert_fusion.flags_ref, bf16[192,384]{1,0:T(8,128)(2,1)} %get-tuple-element.134.refs_0_.above_ref, bf16[192,384]{1,0:T(8,128)(2,1)} %get-tuple-element.76.refs_1_.mid_ref, ...), custom_call_target="tpu_custom_call" | custom-call | flops 1000000000 | bytes 2932748 | tf_op jit(solution)/shard_map/in_weight/pallas_call | solution.py:67
  104.9 1.4 collective-permute-done.6.refs_1_
  106.3 4.5 %collective-permute-start.7 = (bf16[96,384]{1,0:T(8,128)(2,1)S(1)}, bf16[96,384]{1,0:T(8,128)(2,1)S(1)}, u32[]{:S(2)}, u32[]{:S(2)}) collective-permute-start(bf16[96,384]{1,0:T(8,128)(2,1)S(1)} %copy-done.14), channel_id=1, source_target_pairs={{8,0},{16,8},{24,16},{32,24},{40,32},{48,40},{56,48},{64,56},{72,6... | collective-permute-start | bytes 221192 | tf_op jit(solution)/shard_map/ppermute | solution.py:684
  112.9 3.4 %close.3 = (f32[96,1536]{1,0:T(8,128)}, f32[48,256]{1,0:T(8,128)}, f32[48,256]{1,0:T(8,128)}) custom-call(s32[1]{0:T(128)} %bitcast.6.core_ref, f32[2]{0:T(128)} %add_convert_fusion.flags_ref, f32[192,384]{1,0:T(8,128)} %get-tuple-element.99.refs_0_, bf16[96,384]{1,0:T(8,128)(2,1)} %copy-done.15, bf16[96,384]{1,0:T(8,128)(2,1)} %copy-done.17, ...), custom_call_target="tpu_custom_call" | custom-call | flops 1000000000 | bytes 2718732 | tf_op jit(solution)/shard_map/close/pallas_call | solution.py:67
  119.6 3.9 %merge.1 = bf16[64,88,128]{2,1,0:T(8,128)(2,1)} custom-call(f32[224,512]{1,0:T(8,128)} %get-tuple-element.109.refs_0_, f32[3,144,512]{2,1,0:T(8,128)} %get-tuple-element.110.refs_1_, f32[48,256]{1,0:T(8,128)} %get-tuple-element.111.refs_2_, f32[224,512]{1,0:T(8,128)} %copy-done.6, f32[3,144,512]{2,1,0:T(8,128)} %copy-done.4, f32[48,256]{1,0:T(8,128)} %copy-done.9, ...), custom_call_target="tpu_custom_call" | custom-call | bytes 7012352 | tf_op jit(solution)/shard_map/merge/pallas_call | solution.py:67
  123.6 32.6 %all_to_all.15.shares_ref = bf16[64,88,128]{2,1,0:T(8,128)(2,1)} all-to-all(bf16[64,88,128]{2,1,0:T(8,128)(2,1)} %merge.1), channel_id=1, replica_groups=mesh['y'=4,'xl'=2,'c'=2,'z'=4,'xh'=2] {'y','xl','z','xh'}, dimensions={0} | all-to-all | bytes 2883584 | tf_op jit(solution)/shard_map/all_to_all | solution.py:692
  156.2 2.7 %totals.1 = bf16[64,88,128]{2,1,0:T(8,128)(2,1)} custom-call(bf16[64,88,128]{2,1,0:T(8,128)(2,1)} %all_to_all.15.shares_ref), custom_call_target="tpu_custom_call" | custom-call | bytes 2883584 | tf_op jit(solution)/shard_map/totals/pallas_call | solution.py:67
  158.9 24.8 %all_to_all.16.mine_ref = bf16[64,88,128]{2,1,0:T(8,128)(2,1)S(1)} all-to-all(bf16[64,88,128]{2,1,0:T(8,128)(2,1)} %totals.1), channel_id=1, replica_groups=mesh['y'=4,'xl'=2,'c'=2,'z'=4,'xh'=2] {'y','xl','z','xh'}, dimensions={0} | all-to-all | bytes 2883584 | tf_op jit(solution)/shard_map/all_to_all | solution.py:702
  183.7 4.0 %collective-permute-start.14 = (bf16[64,88,128]{2,1,0:T(8,128)(2,1)S(1)}, bf16[64,88,128]{2,1,0:T(8,128)(2,1)S(1)}, u32[]{:S(2)}, u32[]{:S(2)}) collective-permute-start(bf16[64,88,128]{2,1,0:T(8,128)(2,1)S(1)} %all_to_all.16.mine_ref), channel_id=1, source_target_pairs={{0,8},{8,0},{1,9},{9,1},{2,10},{10,2},{3,11},{11,3},{4,12},{12,4},... | collective-permute-start | bytes 4325384 | tf_op jit(solution)/shard_map/ppermute | solution.py:703
  187.8 2.5 %weave.2 = f32[1,96,2,768]{3,2,1,0:T(2,128)} custom-call(f32[96,1536]{1,0:T(8,128)} %get-tuple-element.83.x_ref.refs_6_), custom_call_target="tpu_custom_call" | custom-call | bytes 1179648 | tf_op jit(solution)/shard_map/weave/pallas_call | solution.py:67
  190.2 2.5 %weave.3 = f32[1,96,2,768]{3,2,1,0:T(2,128)} custom-call(f32[96,1536]{1,0:T(8,128)} %get-tuple-element.107.x_ref), custom_call_target="tpu_custom_call" | custom-call | bytes 1179648 | tf_op jit(solution)/shard_map/weave/pallas_call | solution.py:67
  192.7 1.1 copy-done.2
  193.9 4.8 %unpack.1 = (f32[2,432,512]{2,1,0:T(8,128)}, f32[2,9,96,512]{3,2,1,0:T(8,128)}, f32[2,96,96]{2,1,0:T(8,128)}, f32[2,512]{1,0:T(2,128)}, f32[2,8,96]{2,1,0:T(8,128)}) custom-call(s32[1]{0:T(128)} %bitcast.6.core_ref, bf16[64,88,128]{2,1,0:T(8,128)(2,1)} %copy-done, bf16[64,88,128]{2,1,0:T(8,128)(2,1)} %copy-done.2), custom_call_target="tpu_custom_call" | custom-call | bytes 8275972 | tf_op jit(solution)/shard_map/unpack/pallas_call | solution.py:67
  198.7 1.3 slice.35
  (66 shorter events, 13.2 us)
Async XLA Ops:
  0.6 9.2 %copy-start.7 = (f32[1,192,1,384]{3,2,1,0:T(1,128)S(1)}, f32[1,192,1,384]{3,2,1,0:T(1,128)}, u32[]{:S(2)}) copy-start(f32[1,192,1,384]{3,2,1,0:T(1,128)} %param.10) | copy-start | bytes 884740
  2.9 21.0 %all-to-all-start = ((bf16[16,24,1152]{2,1,0:T(8,128)(2,1)}), bf16[16,24,1152]{2,1,0:T(8,128)(2,1)S(1)}, u32[]{:S(2)}, u32[]{:S(2)}) async-start(bf16[16,24,1152]{2,1,0:T(8,128)(2,1)} %payload.1), calls=%async_computation | async-start | bytes 1769472 | tf_op jit(solution)/shard_map/all_to_all | solution.py:650
  23.9 0.9 copy-start.1
  38.7 13.1 %collective-permute-start = (bf16[384,384]{1,0:T(8,128)(2,1)}, bf16[384,384]{1,0:T(8,128)(2,1)S(1)}, u32[]{:S(2)}, u32[]{:S(2)}) collective-permute-start(bf16[384,384]{1,0:T(8,128)(2,1)} %get-tuple-element.75), channel_id=1, source_target_pairs={{0,8},{8,16},{16,24},{24,32},{32,40},{40,48},{48,56},{56,64},{64,7... | collective-permute-start | bytes 884744 | tf_op jit(solution)/shard_map/ppermute | solution.py:659
  39.9 12.6 %collective-permute-start.1 = (bf16[384,384]{1,0:T(8,128)(2,1)}, bf16[384,384]{1,0:T(8,128)(2,1)S(1)}, u32[]{:S(2)}, u32[]{:S(2)}) collective-permute-start(bf16[384,384]{1,0:T(8,128)(2,1)} %get-tuple-element.77), channel_id=1, source_target_pairs={{8,0},{16,8},{24,16},{32,24},{40,32},{48,40},{56,48},{64,56},{72,6... | collective-permute-start | bytes 884744 | tf_op jit(solution)/shard_map/ppermute | solution.py:660
  48.2 69.9 %collective-permute-start.12 = (f32[3,144,512]{2,1,0:T(8,128)}, f32[3,144,512]{2,1,0:T(8,128)S(1)}, u32[]{:S(2)}, u32[]{:S(2)}) collective-permute-start(f32[3,144,512]{2,1,0:T(8,128)} %get-tuple-element.120), channel_id=1, source_target_pairs={{0,8},{8,0},{1,9},{9,1},{2,10},{10,2},{3,11},{11,3},{4,12},{12,4},... | collective-permute-start | bytes 2654216 | tf_op jit(solution)/shard_map/ppermute | solution.py:667
  60.8 18.4 %collective-permute-start.2 = (bf16[96,384]{1,0:T(8,128)(2,1)}, bf16[96,384]{1,0:T(8,128)(2,1)S(1)}, u32[]{:S(2)}, u32[]{:S(2)}) collective-permute-start(bf16[96,384]{1,0:T(8,128)(2,1)} %get-tuple-element.88), channel_id=1, source_target_pairs={{0,8},{8,16},{16,24},{24,32},{32,40},{40,48},{48,56},{56,64},{64,7... | collective-permute-start | bytes 221192 | tf_op jit(solution)/shard_map/ppermute | solution.py:665
  60.8 18.5 %collective-permute-start.3 = (bf16[96,384]{1,0:T(8,128)(2,1)}, bf16[96,384]{1,0:T(8,128)(2,1)S(1)}, u32[]{:S(2)}, u32[]{:S(2)}) collective-permute-start(bf16[96,384]{1,0:T(8,128)(2,1)} %get-tuple-element.89), channel_id=1, source_target_pairs={{8,0},{16,8},{24,16},{32,24},{40,32},{48,40},{56,48},{64,56},{72,6... | collective-permute-start | bytes 221192 | tf_op jit(solution)/shard_map/ppermute | solution.py:666
  65.0 53.2 %collective-permute-start.11 = (f32[224,512]{1,0:T(8,128)}, f32[224,512]{1,0:T(8,128)S(1)}, u32[]{:S(2)}, u32[]{:S(2)}) collective-permute-start(f32[224,512]{1,0:T(8,128)} %get-tuple-element.119), channel_id=1, source_target_pairs={{0,8},{8,0},{1,9},{9,1},{2,10},{10,2},{3,11},{11,3},{4,12},{12,4},... | collective-permute-start | bytes 1376264 | tf_op jit(solution)/shard_map/ppermute | solution.py:679
  84.4 8.2 %collective-permute-start.5 = (bf16[192,384]{1,0:T(8,128)(2,1)S(1)}, bf16[192,384]{1,0:T(8,128)(2,1)S(1)}, u32[]{:S(2)}, u32[]{:S(2)}) collective-permute-start(bf16[192,384]{1,0:T(8,128)(2,1)S(1)} %get-tuple-element.129), channel_id=1, source_target_pairs={{8,0},{16,8},{24,16},{32,24},{40,32},{48,40},{56,48},{64,56},{72,6... | collective-permute-start | bytes 442376 | tf_op jit(solution)/shard_map/ppermute | solution.py:676
  84.4 8.1 %collective-permute-start.4 = (bf16[192,384]{1,0:T(8,128)(2,1)S(1)}, bf16[192,384]{1,0:T(8,128)(2,1)S(1)}, u32[]{:S(2)}, u32[]{:S(2)}) collective-permute-start(bf16[192,384]{1,0:T(8,128)(2,1)S(1)} %get-tuple-element.130), channel_id=1, source_target_pairs={{0,8},{8,16},{16,24},{24,32},{32,40},{40,48},{48,56},{56,64},{64,7... | collective-permute-start | bytes 442376 | tf_op jit(solution)/shard_map/ppermute | solution.py:675
  92.5 25.7 %collective-permute-start.9 = (f32[3,144,512]{2,1,0:T(8,128)}, f32[3,144,512]{2,1,0:T(8,128)S(1)}, u32[]{:S(2)}, u32[]{:S(2)}) collective-permute-start(f32[3,144,512]{2,1,0:T(8,128)} %get-tuple-element.113), channel_id=1, source_target_pairs={{0,8},{8,0},{1,9},{9,1},{2,10},{10,2},{3,11},{11,3},{4,12},{12,4},... | collective-permute-start | bytes 2654216 | tf_op jit(solution)/shard_map/ppermute | solution.py:681
  92.5 0.7 copy-start.10
  92.5 0.7 copy-start.11
  100.7 4.2 %copy-start.16 = (bf16[96,384]{1,0:T(8,128)(2,1)S(1)}, bf16[96,384]{1,0:T(8,128)(2,1)}, u32[]{:S(2)}) copy-start(bf16[96,384]{1,0:T(8,128)(2,1)} %get-tuple-element.100) | copy-start | bytes 221188
  100.7 5.6 %copy-start.14 = (bf16[96,384]{1,0:T(8,128)(2,1)S(1)}, bf16[96,384]{1,0:T(8,128)(2,1)}, u32[]{:S(2)}) copy-start(bf16[96,384]{1,0:T(8,128)(2,1)} %get-tuple-element.101) | copy-start | bytes 221188
  100.7 11.1 %copy-start.18 = (f32[48,256]{1,0:T(8,128)S(1)}, f32[48,256]{1,0:T(8,128)}, u32[]{:S(2)}) copy-start(f32[48,256]{1,0:T(8,128)} %get-tuple-element.121) | copy-start | bytes 147460
  104.4 13.7 %collective-permute-start.8 = (f32[224,512]{1,0:T(8,128)}, f32[224,512]{1,0:T(8,128)S(1)}, u32[]{:S(2)}, u32[]{:S(2)}) collective-permute-start(f32[224,512]{1,0:T(8,128)} %get-tuple-element.112), channel_id=1, source_target_pairs={{0,8},{8,0},{1,9},{9,1},{2,10},{10,2},{3,11},{11,3},{4,12},{12,4},... | collective-permute-start | bytes 1376264 | tf_op jit(solution)/shard_map/ppermute | solution.py:686
  104.9 1.4 collective-permute-start.6
  106.3 6.5 %copy-start.15 = (bf16[96,384]{1,0:T(8,128)(2,1)}, bf16[96,384]{1,0:T(8,128)(2,1)S(1)}, u32[]{:S(2)}) copy-start(bf16[96,384]{1,0:T(8,128)(2,1)S(1)} %collective-permute-done.6.refs_1_) | copy-start | bytes 221188
  106.3 5.5 %collective-permute-start.7 = (bf16[96,384]{1,0:T(8,128)(2,1)S(1)}, bf16[96,384]{1,0:T(8,128)(2,1)S(1)}, u32[]{:S(2)}, u32[]{:S(2)}) collective-permute-start(bf16[96,384]{1,0:T(8,128)(2,1)S(1)} %copy-done.14), channel_id=1, source_target_pairs={{8,0},{16,8},{24,16},{32,24},{40,32},{48,40},{56,48},{64,56},{72,6... | collective-permute-start | bytes 221192 | tf_op jit(solution)/shard_map/ppermute | solution.py:684
  111.8 1.1 copy-start.17
  111.8 4.5 %collective-permute-start.13 = (f32[48,256]{1,0:T(8,128)S(1)}, f32[48,256]{1,0:T(8,128)S(1)}, u32[]{:S(2)}, u32[]{:S(2)}) collective-permute-start(f32[48,256]{1,0:T(8,128)S(1)} %copy-done.18), channel_id=1, source_target_pairs={{0,8},{8,0},{1,9},{9,1},{2,10},{10,2},{3,11},{11,3},{4,12},{12,4},... | collective-permute-start | bytes 147464 | tf_op jit(solution)/shard_map/ppermute | solution.py:680
  116.3 1.9 copy-start.8
  116.3 1.8 collective-permute-start.10
  118.1 0.8 copy-start.5
  118.1 1.1 copy-start.3
  118.2 1.2 copy-start.6
  118.2 1.5 copy-start.4
  183.7 9.0 %copy-start = (bf16[64,88,128]{2,1,0:T(8,128)(2,1)}, bf16[64,88,128]{2,1,0:T(8,128)(2,1)S(1)}, u32[]{:S(2)}) copy-start(bf16[64,88,128]{2,1,0:T(8,128)(2,1)S(1)} %all_to_all.16.mine_ref) | copy-start | bytes 4325380
  183.7 9.0 %collective-permute-start.14 = (bf16[64,88,128]{2,1,0:T(8,128)(2,1)S(1)}, bf16[64,88,128]{2,1,0:T(8,128)(2,1)S(1)}, u32[]{:S(2)}, u32[]{:S(2)}) collective-permute-start(bf16[64,88,128]{2,1,0:T(8,128)(2,1)S(1)} %all_to_all.16.mine_ref), channel_id=1, source_target_pairs={{0,8},{8,0},{1,9},{9,1},{2,10},{10,2},{3,11},{11,3},{4,12},{12,4},... | collective-permute-start | bytes 4325384 | tf_op jit(solution)/shard_map/ppermute | solution.py:703
  192.7 1.1 copy-start.2
  (3 other events, 1.9 us)
